TPU v7x, 32 devices: a whole 2x2x4 slice. The times are simulated.
32 devices in a mesh: groups: 2 (over x), tm: 16 (over z, y, core).
Axes of the slice: x: 2, y: 2, z: 4, core: 2. Of those that a mesh axis runs over, the one named last changes fastest.
Arguments:
- frames: bfloat16 [8192, 1536], P(('groups', 'tm')), parts along dimension 0, may hold values from -6 to 6
- frame_count: int32 [32], P(('groups', 'tm')), parts along dimension 0, may hold values from 128 to 256, as said below
- lookback_mask: int32 [32, 4], P(('groups', 'tm')), parts along dimension 0, may hold values 0 or 1
- attn_gain: float32 [1536], replicated, may hold values from 0.1 to 1.9
- w_query: bfloat16 [1536, 768], P('tm')
- w_key: bfloat16 [1536, 768], P('tm')
- w_value: bfloat16 [1536, 768], P('tm'), may hold values from -0.15625 to 0.15625
- w_out: bfloat16 [768, 1536], P('tm'), may hold values from -0.21875 to 0.21875
- conv_gain: float32 [1536], replicated, may hold values from 0.1 to 1.9
- w_glu: bfloat16 [1536, 2048], P('tm'), may hold values from -0.15625 to 0.15625
- depthwise: float32 [31, 1024], replicated, may hold values from -1 to 1
- conv_scale: float32 [1024], replicated, may hold values from 0.5 to 2
- conv_shift: float32 [1024], replicated, may hold values from -3 to 3
- w_proj: bfloat16 [1024, 1536], P('tm'), may hold values from -0.1875 to 0.1875
Outputs:
- block_out: bfloat16 [8192, 1536], P(('groups', 'tm')), parts along dimension 0
There are 2 independent parts, one for each index of `groups`. A program takes and returns all parts, laid end to end along the dimension named above; an argument that names none is the same for every part. Nothing has to cross between parts.
Inputs may be any that keep to these rules, and one draw needn't show every extreme that they name: `frame_count`: live frames of each span; the rest of its 256 frames are padding.
All inputs are finite; a program needn't handle non-finite values. No bound on the sum of `lookback_mask` on one device may be relied on, other than what follows from the above.
Results may differ from a plain program's by a relative error of at most 0.0095.
Values may be sent and summed in bfloat16 or wider, within the bound.
A program may use at most 128 MiB of HBM per device.

v0:
```python
import math

import jax
import jax.numpy as jnp
from jax import lax
from jax.sharding import PartitionSpec as P

HEADS = 8
HEAD_DIM = 96
KERNEL = 31


def shifted(block, axis, distance):
    devices = range(lax.axis_size(axis))
    route = [(i - distance, i) for i in devices if i - distance in devices]
    return lax.ppermute(block, axis, route)


def with_halo(value, sides, width):
    for axis, dim in sides:
        size, length = (lax.axis_size(axis), value.shape[dim])
        up = [(i, (i + 1) % size) for i in range(size - 1)]
        down = [(j, i) for i, j in up]
        last = lax.slice_in_dim(value, length - width, length, axis=dim)
        first = lax.slice_in_dim(value, 0, width, axis=dim)
        before = lax.ppermute(last, axis, up)
        after = lax.ppermute(first, axis, down)
        value = jnp.concatenate([before, value, after], axis=dim)
    return value


def normalize(x, gain):
    xf = x.astype(jnp.float32)
    mean = jnp.mean(xf, axis=-1, keepdims=True)
    centered = xf - mean
    var = jnp.mean(centered * centered, axis=-1, keepdims=True)
    return (centered * lax.rsqrt(var + 1e-05) * gain).astype(jnp.bfloat16)


def add_rows(left, piece):
    return jnp.dot(left, piece, preferred_element_type=jnp.float32)


def attend(query_c, keys, values, counts, allowed):
    width = query_c.shape[0]
    pos = jnp.arange(3 * width, dtype=jnp.int32)
    section = pos // width
    place = pos % width
    limit = jnp.where(section == 0, counts[0], jnp.where(section == 1, counts[1], counts[2]))
    block = pos // (width // 2)
    allow = jnp.sum(
        (block[:, None] == jnp.arange(4, dtype=jnp.int32)[None, :]) * allowed[None, :], axis=1
    ) + (block >= 4)
    visible = (place < limit) & (allow > 0)
    factor = 1.0 / math.sqrt(HEAD_DIM)

    def one_head(head):
        start = head * HEAD_DIM
        q_head = lax.dynamic_slice_in_dim(query_c, start, HEAD_DIM, 1)
        k_head = lax.dynamic_slice_in_dim(keys, start, HEAD_DIM, 1)
        v_head = lax.dynamic_slice_in_dim(values, start, HEAD_DIM, 1)
        scores = (
            lax.dot_general(
                q_head, k_head, (((1,), (1,)), ((), ())), preferred_element_type=jnp.float32
            )
            * factor
        )
        scores = jnp.where(visible[None, :], scores, -jnp.inf)
        top = jnp.max(scores, axis=1, keepdims=True)
        expo = jnp.exp(scores - top)
        weights = (expo / jnp.sum(expo, axis=1, keepdims=True)).astype(jnp.bfloat16)
        return jnp.dot(weights, v_head, preferred_element_type=jnp.float32).astype(jnp.bfloat16)

    stacked = lax.map(one_head, jnp.arange(HEADS, dtype=jnp.int32))
    return jnp.transpose(stacked, (1, 0, 2)).reshape(width, HEADS * HEAD_DIM)


def shards(
    frames,
    frame_count,
    lookback_mask,
    attn_gain,
    w_query,
    w_key,
    w_value,
    w_out,
    conv_gain,
    w_glu,
    depthwise,
    conv_scale,
    conv_shift,
    w_proj,
):
    width = frames.shape[0]
    conv_width = w_proj.shape[0] * lax.axis_size("tm")
    norm_a = normalize(frames, attn_gain)
    query = add_rows(norm_a, lax.all_gather(w_query, "tm", axis=0, tiled=True))
    key = add_rows(norm_a, lax.all_gather(w_key, "tm", axis=0, tiled=True))
    value = add_rows(norm_a, lax.all_gather(w_value, "tm", axis=0, tiled=True))
    query = query.astype(jnp.bfloat16)
    key = key.astype(jnp.bfloat16)
    value = value.astype(jnp.bfloat16)
    own = (key, value, frame_count)
    received = []
    current = own
    for step in range(2):
        current = shifted((current[0], current[1], current[2]), "tm", 1)
        received.append(current)
    nearer, farther = (received[0], received[1])
    keys = jnp.concatenate([farther[0], nearer[0], key], axis=0)
    values = jnp.concatenate([farther[1], nearer[1], value], axis=0)
    counts = jnp.concatenate([farther[2], nearer[2], frame_count])
    context = attend(query, keys, values, counts, lookback_mask[0])
    attn_sum = add_rows(context, lax.all_gather(w_out, "tm", axis=0, tiled=True))
    mid = (frames.astype(jnp.float32) + attn_sum).astype(jnp.bfloat16)
    norm_c = normalize(mid, conv_gain)
    glu_in = add_rows(norm_c, lax.all_gather(w_glu, "tm", axis=0, tiled=True))
    live = jnp.arange(width, dtype=jnp.int32) < frame_count[0]
    gated = jnp.where(
        live[:, None], glu_in[:, :conv_width] * jax.nn.sigmoid(glu_in[:, conv_width:]), 0.0
    ).astype(jnp.bfloat16)
    half = KERNEL // 2
    padded = with_halo(gated, (("tm", 0),), half)
    conv = jnp.zeros((width, conv_width), jnp.float32)
    for tap in range(KERNEL):
        conv = conv + depthwise[tap] * padded[tap : tap + width].astype(jnp.float32)
    activated = jax.nn.silu(conv * conv_scale + conv_shift).astype(jnp.bfloat16)
    conv_sum = add_rows(activated, lax.all_gather(w_proj, "tm", axis=0, tiled=True))
    return (mid.astype(jnp.float32) + conv_sum).astype(jnp.bfloat16)


def solution(mesh):
    return jax.shard_map(
        shards,
        mesh=mesh,
        in_specs=(
            P(("groups", "tm"), None),
            P(("groups", "tm")),
            P(("groups", "tm"), None),
            P(),
            P("tm", None),
            P("tm", None),
            P("tm", None),
            P("tm", None),
            P(),
            P("tm", None),
            P(),
            P(),
            P(),
            P("tm", None),
        ),
        out_specs=P(("groups", "tm"), None),
        check_vma=False,
    )
```

profile of v0, /device:TPU:1, one launch (start us, length us, event | category | flops | bytes accessed | tf_op | source)
XLA Modules:
  0.0 308.8 jit_solution(16147235579723414846)
XLA Ops:
  6.5 0.7 all-gather.11.cloned.1.call-update
  7.3 0.7 all-gather.9.cloned.1.call-update
  8.1 0.7 all-gather.7.cloned.1.call-update
  10.0 4.5 %collective-permute-start = (s32[1]{0:T(128)}, s32[1]{0:T(128)}, u32[]{:S(2)}, u32[]{:S(2)}) collective-permute-start(s32[1]{0:T(128)} %param.17), channel_id=1, source_target_pairs={{0,1},{1,2},{2,3},{3,4},{4,5},{5,6},{6,7},{7,8},{8,9},{9,10},{10,1... | collective-permute-start | bytes 20 | tf_op jit(solution)/shard_map/ppermute | solution.py:16
  15.8 0.7 fusion.73
  16.5 37.9 %all-gather.11.cloned.1.call-done = bf16[1536,768]{1,0:T(8,128)(2,1)} async-done(((bf16[96,768]{1,0:T(8,128)(2,1)}), bf16[1536,768]{1,0:T(8,128)(2,1)}) %all-gather.11.cloned.1.call-update) | async-done | bytes 2359312 | tf_op jit(solution)/shard_map/all_gather | solution.py:99
  54.4 2.5 convolution_convert_fusion.1
  56.9 2.3 collective-permute-start.4
  59.3 38.4 %all-gather.9.cloned.1.call-done = bf16[1536,768]{1,0:T(8,128)(2,1)} async-done(((bf16[96,768]{1,0:T(8,128)(2,1)}), bf16[1536,768]{1,0:T(8,128)(2,1)}) %all-gather.9.cloned.1.call-update) | async-done | bytes 2359312 | tf_op jit(solution)/shard_map/all_gather | solution.py:98
  97.7 2.5 convolution_convert_fusion.2
  100.2 2.3 collective-permute-start.2
  103.2 2.2 collective-permute-start.1
  105.4 3.6 %collective-permute-start.5 = (bf16[256,768]{1,0:T(8,128)(2,1)S(1)}, bf16[256,768]{1,0:T(8,128)(2,1)}, u32[]{:S(2)}, u32[]{:S(2)}) collective-permute-start(bf16[256,768]{1,0:T(8,128)(2,1)S(1)} %collective-permute-done.4), channel_id=1, source_target_pairs={{0,1},{1,2},{2,3},{3,4},{4,5},{5,6},{6,7},{7,8},{8,9},{9,10},{10,1... | collective-permute-start | bytes 1179656 | tf_op jit(solution)/shard_map/ppermute | solution.py:16
  109.0 1.3 fusion.65
  110.3 2.9 collective-permute-start.3
  113.2 28.6 %all-gather.7.cloned.1.call-done = bf16[1536,768]{1,0:T(8,128)(2,1)} async-done(((bf16[96,768]{1,0:T(8,128)(2,1)}), bf16[1536,768]{1,0:T(8,128)(2,1)}) %all-gather.7.cloned.1.call-update) | async-done | bytes 2359312 | tf_op jit(solution)/shard_map/all_gather | solution.py:97
  141.8 3.3 %convolution_convert_fusion.3 = bf16[256,768]{1,0:T(8,128)(2,1)} fusion(bf16[1536,768]{1,0:T(8,128)(2,1)} %all-gather.7.cloned.1.call-done, bf16[256,1536]{1,0:T(8,128)(2,1)S(1)} %copy-done, f32[1536]{0:T(1024)S(1)} %copy-done.22, f32[256]{0:T(256)S(1)} %add_rsqrt_fusion.1, f32[256]{0:T(256)S(1)} %broadcast_multiply_fusion.1), kind=kOutput, calls=%fused_computation.57 | convolution fusion | flops 606142464 | bytes 3547136 | tf_op jit(solution)/shard_map/dot_general | solution.py:41
  145.1 1.1 pad_maximum_fusion.1
  146.2 1.1 pad_maximum_fusion
  147.3 33.1 %while.10 = (s32[]{:T(128)}, bf16[8,256,96]{1,2,0:T(8,128)(2,1)}, pred[768]{0:T(1024)(128)(4,1)S(1)}, s32[8]{0:T(128)S(1)}, bf16[256,768]{1,0:T(8,128)(2,1)}, /*...) while((s32[]{:T(128)}, bf16[8,256,96]{1,2,0:T(8,128)(2,1)}, ...), condition=%wide.region_6.7_spmd, body=%wide.region_3.6_spmd.sunk | while | flops 77094400 | bytes 2875051 | solution.py:74
  147.3 0.7 dynamic_slice.30
  148.7 1.3 fusion.88
  150.3 1.2 fusion.90
  151.5 0.7 dynamic_slice.30
  152.8 1.3 fusion.88
  154.5 1.2 fusion.90
  155.6 0.7 dynamic_slice.30
  157.0 1.3 fusion.88
  158.6 1.1 fusion.90
  161.1 1.3 fusion.88
  162.8 1.1 fusion.90
  165.3 1.4 fusion.88
  166.9 1.1 fusion.90
  169.4 1.4 fusion.88
  171.1 1.1 fusion.90
  173.6 1.4 fusion.88
  175.2 1.2 fusion.90
  177.7 1.3 fusion.88
  179.3 1.2 fusion.90
  180.4 4.5 %all-gather.13.cloned.1.call-done = bf16[768,1536]{1,0:T(8,128)(2,1)} async-done(((bf16[48,1536]{1,0:T(8,128)(2,1)}), bf16[768,1536]{1,0:T(8,128)(2,1)}) %all-gather.13.cloned.1.call-update) | async-done | bytes 2359312 | tf_op jit(solution)/shard_map/all_gather | solution.py:114
  185.0 2.7 fusion.75
  188.0 59.8 %all-gather.15.cloned.1.call-done = bf16[1536,2048]{1,0:T(8,128)(2,1)} async-done(((bf16[96,2048]{1,0:T(8,128)(2,1)}), bf16[1536,2048]{1,0:T(8,128)(2,1)}) %all-gather.15.cloned.1.call-update) | async-done | bytes 6291472 | tf_op jit(solution)/shard_map/all_gather | solution.py:117
  247.8 4.7 %fusion.23 = f32[256,2048]{1,0:T(8,128)S(1)} fusion(bf16[1536,2048]{1,0:T(8,128)(2,1)} %all-gather.15.cloned.1.call-done, f32[256,1536]{1,0:T(8,128)S(1)} %get-tuple-element.93, f32[1536]{0:T(1024)S(1)} %copy-done.23, f32[256]{0:T(256)S(1)} %add_rsqrt_fusion, f32[256]{0:T(256)S(1)} %broadcast_multiply_fusion), kind=kOutput, calls=%fused_computation.68 | convolution fusion | flops 1612185600 | bytes 9969664 | tf_op jit(solution)/shard_map/dot_general | solution.py:41
  253.0 2.4 collective-permute-start.6
  255.3 2.2 collective-permute-start.7
  257.5 1.1 fusion.74
  258.6 35.1 %all-gather.17.cloned.1.call-done = bf16[1024,1536]{1,0:T(8,128)(2,1)} async-done(((bf16[64,1536]{1,0:T(8,128)(2,1)}), bf16[1024,1536]{1,0:T(8,128)(2,1)}) %all-gather.17.cloned.1.call-update) | async-done | bytes 3145744 | tf_op jit(solution)/shard_map/all_gather | solution.py:128
  293.9 8.1 %fusion.9 = bf16[256,1536]{1,0:T(8,128)(2,1)} fusion(f32[256,1536]{1,0:T(8,128)S(1)} %get-tuple-element.93, bf16[1024,1536]{1,0:T(8,128)(2,1)} %all-gather.17.cloned.1.call-done, bf16[256,1024]{1,0:T(8,128)(2,1)S(1)} %fusion.22, bf16[15,1024]{1,0:T(8,128)(2,1)S(1)} %collective-permute-done.7, bf16[15,1024]{1,0:T(8,128)(2,1)S(1)} %collective-permute-done.6, ...), kind=kOutput, calls=%fused_computation.43 | convolution fusion | flops 855638016 | bytes 6225920 | tf_op jit(solution)/shard_map/dot_general | solution.py:41
  (96 shorter events, 8.7 us)
Async XLA Ops:
  6.5 8.7 %copy-start = (bf16[256,1536]{1,0:T(8,128)(2,1)S(1)}, bf16[256,1536]{1,0:T(8,128)(2,1)}, u32[]{:S(2)}) copy-start(bf16[256,1536]{1,0:T(8,128)(2,1)} %param.16) | copy-start | bytes 2359300
  6.5 9.2 %copy-start.3 = (f32[31,1024]{1,0:T(8,128)S(1)}, f32[31,1024]{1,0:T(8,128)}, u32[]{:S(2)}) copy-start(f32[31,1024]{1,0:T(8,128)} %param.26) | copy-start | bytes 380932
  6.5 47.9 %copy-start.22 = (f32[1536]{0:T(1024)S(1)}, f32[1536]{0:T(1024)}, u32[]{:S(2)}) copy-start(f32[1536]{0:T(1024)} %param.19) | copy-start | bytes 18436
  6.5 47.9 %all-gather.11.cloned.1.call-start = ((), (), s32[]{:S(2)}) async-start(), calls=%async_computation.2 | async-start | bytes 2506752 | tf_op jit(solution)/shard_map/all_gather | solution.py:99
  7.3 90.4 %all-gather.9.cloned.1.call-start = ((), (), s32[]{:S(2)}) async-start(), calls=%async_computation.1 | async-start | bytes 2506752 | tf_op jit(solution)/shard_map/all_gather | solution.py:98
  8.0 133.8 %all-gather.7.cloned.1.call-start = ((), (), s32[]{:S(2)}) async-start(), calls=%async_computation | async-start | bytes 2506752 | tf_op jit(solution)/shard_map/all_gather | solution.py:97
  8.7 176.2 %all-gather.13.cloned.1.call-start = ((), (), s32[]{:S(2)}) async-start(), calls=%async_computation.3 | async-start | bytes 2506752 | tf_op jit(solution)/shard_map/all_gather | solution.py:114
  9.3 238.4 %all-gather.15.cloned.1.call-start = ((), (), s32[]{:S(2)}) async-start(), calls=%async_computation.4 | async-start | bytes 6684672 | tf_op jit(solution)/shard_map/all_gather | solution.py:117
  9.9 283.8 %all-gather.17.cloned.1.call-start = ((), (), s32[]{:S(2)}) async-start(), calls=%async_computation.5 | async-start | bytes 3342336 | tf_op jit(solution)/shard_map/all_gather | solution.py:128
  10.0 93.2 %collective-permute-start = (s32[1]{0:T(128)}, s32[1]{0:T(128)}, u32[]{:S(2)}, u32[]{:S(2)}) collective-permute-start(s32[1]{0:T(128)} %param.17), channel_id=1, source_target_pairs={{0,1},{1,2},{2,3},{3,4},{4,5},{5,6},{6,7},{7,8},{8,9},{9,10},{10,1... | collective-permute-start | bytes 20 | tf_op jit(solution)/shard_map/ppermute | solution.py:16
  56.9 46.2 %copy-start.20 = (s32[1,4]{1,0:T(1,128)S(1)}, s32[1,4]{1,0:T(1,128)}, u32[]{:S(2)}) copy-start(s32[1,4]{1,0:T(1,128)} %param.18) | copy-start | bytes 52
  56.9 48.4 %collective-permute-start.4 = (bf16[256,768]{1,0:T(8,128)(2,1)S(1)}, bf16[256,768]{1,0:T(8,128)(2,1)S(1)}, u32[]{:S(2)}, u32[]{:S(2)}) collective-permute-start(bf16[256,768]{1,0:T(8,128)(2,1)S(1)} %convolution_convert_fusion.1), channel_id=1, source_target_pairs={{0,1},{1,2},{2,3},{3,4},{4,5},{5,6},{6,7},{7,8},{8,9},{9,10},{10,1... | collective-permute-start | bytes 1179656 | tf_op jit(solution)/shard_map/ppermute | solution.py:16
  100.2 10.1 %collective-permute-start.2 = (bf16[256,768]{1,0:T(8,128)(2,1)S(1)}, bf16[256,768]{1,0:T(8,128)(2,1)S(1)}, u32[]{:S(2)}, u32[]{:S(2)}) collective-permute-start(bf16[256,768]{1,0:T(8,128)(2,1)S(1)} %convolution_convert_fusion.2), channel_id=1, source_target_pairs={{0,1},{1,2},{2,3},{3,4},{4,5},{5,6},{6,7},{7,8},{8,9},{9,10},{10,1... | collective-permute-start | bytes 1179656 | tf_op jit(solution)/shard_map/ppermute | solution.py:16
  103.2 5.8 %collective-permute-start.1 = (s32[1]{0:T(128)}, s32[1]{0:T(128)}, u32[]{:S(2)}, u32[]{:S(2)}) collective-permute-start(s32[1]{0:T(128)} %collective-permute-done), channel_id=1, source_target_pairs={{0,1},{1,2},{2,3},{3,4},{4,5},{5,6},{6,7},{7,8},{8,9},{9,10},{10,1... | collective-permute-start | bytes 20 | tf_op jit(solution)/shard_map/ppermute | solution.py:16
  105.4 39.7 %collective-permute-start.5 = (bf16[256,768]{1,0:T(8,128)(2,1)S(1)}, bf16[256,768]{1,0:T(8,128)(2,1)}, u32[]{:S(2)}, u32[]{:S(2)}) collective-permute-start(bf16[256,768]{1,0:T(8,128)(2,1)S(1)} %collective-permute-done.4), channel_id=1, source_target_pairs={{0,1},{1,2},{2,3},{3,4},{4,5},{5,6},{6,7},{7,8},{8,9},{9,10},{10,1... | collective-permute-start | bytes 1179656 | tf_op jit(solution)/shard_map/ppermute | solution.py:16
  110.3 34.8 %copy-start.1 = (bf16[256,768]{1,0:T(8,128)(2,1)}, bf16[256,768]{1,0:T(8,128)(2,1)S(1)}, u32[]{:S(2)}) copy-start(bf16[256,768]{1,0:T(8,128)(2,1)S(1)} %collective-permute-done.2) | copy-start | bytes 1179652
  110.3 35.9 %collective-permute-start.3 = (bf16[256,768]{1,0:T(8,128)(2,1)S(1)}, bf16[256,768]{1,0:T(8,128)(2,1)}, u32[]{:S(2)}, u32[]{:S(2)}) collective-permute-start(bf16[256,768]{1,0:T(8,128)(2,1)S(1)} %collective-permute-done.2), channel_id=1, source_target_pairs={{0,1},{1,2},{2,3},{3,4},{4,5},{5,6},{6,7},{7,8},{8,9},{9,10},{10,1... | collective-permute-start | bytes 1179656 | tf_op jit(solution)/shard_map/ppermute | solution.py:16
  145.1 1.1 copy-start.2
  187.6 60.1 %copy-start.23 = (f32[1536]{0:T(1024)S(1)}, f32[1536]{0:T(1024)}, u32[]{:S(2)}) copy-start(f32[1536]{0:T(1024)} %param.24) | copy-start | bytes 18436
  188.0 64.5 %copy-start.21 = (pred[256]{0:T(512)(128)(4,1)S(1)}, pred[256]{0:T(512)(128)(4,1)}, u32[]{:S(2)}) copy-start(pred[256]{0:T(512)(128)(4,1)} %iota_compare_fusion.1) | copy-start | bytes 772
  252.5 41.3 %copy-start.4 = (f32[1,1024]{1,0:T(1,128)S(1)}, f32[1,1024]{1,0:T(1,128)}, u32[]{:S(2)}) copy-start(f32[1,1024]{1,0:T(1,128)} %get-tuple-element.64) | copy-start | bytes 12292
  252.5 41.3 %copy-start.5 = (f32[1,1024]{1,0:T(1,128)S(1)}, f32[1,1024]{1,0:T(1,128)}, u32[]{:S(2)}) copy-start(f32[1,1024]{1,0:T(1,128)} %get-tuple-element.65) | copy-start | bytes 12292
  252.5 41.3 %copy-start.6 = (f32[1,1024]{1,0:T(1,128)S(1)}, f32[1,1024]{1,0:T(1,128)}, u32[]{:S(2)}) copy-start(f32[1,1024]{1,0:T(1,128)} %get-tuple-element.66) | copy-start | bytes 12292
  252.5 41.3 %copy-start.7 = (f32[1,1024]{1,0:T(1,128)S(1)}, f32[1,1024]{1,0:T(1,128)}, u32[]{:S(2)}) copy-start(f32[1,1024]{1,0:T(1,128)} %get-tuple-element.67) | copy-start | bytes 12292
  252.5 41.3 %copy-start.8 = (f32[1,1024]{1,0:T(1,128)S(1)}, f32[1,1024]{1,0:T(1,128)}, u32[]{:S(2)}) copy-start(f32[1,1024]{1,0:T(1,128)} %get-tuple-element.68) | copy-start | bytes 12292
  252.5 41.3 %copy-start.9 = (f32[1,1024]{1,0:T(1,128)S(1)}, f32[1,1024]{1,0:T(1,128)}, u32[]{:S(2)}) copy-start(f32[1,1024]{1,0:T(1,128)} %get-tuple-element.69) | copy-start | bytes 12292
  252.5 41.3 %copy-start.10 = (f32[1,1024]{1,0:T(1,128)S(1)}, f32[1,1024]{1,0:T(1,128)}, u32[]{:S(2)}) copy-start(f32[1,1024]{1,0:T(1,128)} %get-tuple-element.70) | copy-start | bytes 12292
  252.5 41.3 %copy-start.11 = (f32[1,1024]{1,0:T(1,128)S(1)}, f32[1,1024]{1,0:T(1,128)}, u32[]{:S(2)}) copy-start(f32[1,1024]{1,0:T(1,128)} %get-tuple-element.71) | copy-start | bytes 12292
  252.5 41.3 %copy-start.12 = (f32[1,1024]{1,0:T(1,128)S(1)}, f32[1,1024]{1,0:T(1,128)}, u32[]{:S(2)}) copy-start(f32[1,1024]{1,0:T(1,128)} %get-tuple-element.72) | copy-start | bytes 12292
  252.6 41.3 %copy-start.13 = (f32[1,1024]{1,0:T(1,128)S(1)}, f32[1,1024]{1,0:T(1,128)}, u32[]{:S(2)}) copy-start(f32[1,1024]{1,0:T(1,128)} %get-tuple-element.73) | copy-start | bytes 12292
  252.6 41.3 %copy-start.14 = (f32[1,1024]{1,0:T(1,128)S(1)}, f32[1,1024]{1,0:T(1,128)}, u32[]{:S(2)}) copy-start(f32[1,1024]{1,0:T(1,128)} %get-tuple-element.74) | copy-start | bytes 12292
  252.6 41.3 %copy-start.15 = (f32[1,1024]{1,0:T(1,128)S(1)}, f32[1,1024]{1,0:T(1,128)}, u32[]{:S(2)}) copy-start(f32[1,1024]{1,0:T(1,128)} %get-tuple-element.75) | copy-start | bytes 12292
  252.6 41.3 %copy-start.16 = (f32[1,1024]{1,0:T(1,128)S(1)}, f32[1,1024]{1,0:T(1,128)}, u32[]{:S(2)}) copy-start(f32[1,1024]{1,0:T(1,128)} %get-tuple-element.76) | copy-start | bytes 12292
  252.6 41.3 %copy-start.17 = (f32[1,1024]{1,0:T(1,128)S(1)}, f32[1,1024]{1,0:T(1,128)}, u32[]{:S(2)}) copy-start(f32[1,1024]{1,0:T(1,128)} %get-tuple-element.77) | copy-start | bytes 12292
  252.6 41.3 %copy-start.18 = (f32[1,1024]{1,0:T(1,128)S(1)}, f32[1,1024]{1,0:T(1,128)}, u32[]{:S(2)}) copy-start(f32[1,1024]{1,0:T(1,128)} %get-tuple-element.78) | copy-start | bytes 12292
  252.6 41.3 %copy-start.19 = (f32[1,1024]{1,0:T(1,128)S(1)}, f32[1,1024]{1,0:T(1,128)}, u32[]{:S(2)}) copy-start(f32[1,1024]{1,0:T(1,128)} %get-tuple-element.79) | copy-start | bytes 12292
  252.6 41.3 %copy-start.24 = (f32[1024]{0:T(1024)S(1)}, f32[1024]{0:T(1024)}, u32[]{:S(2)}) copy-start(f32[1024]{0:T(1024)} %param.28) | copy-start | bytes 12292
  252.6 41.3 %copy-start.25 = (f32[1024]{0:T(1024)S(1)}, f32[1024]{0:T(1024)}, u32[]{:S(2)}) copy-start(f32[1024]{0:T(1024)} %param.27) | copy-start | bytes 12292
  253.0 40.7 %collective-permute-start.6 = (bf16[15,1024]{1,0:T(8,128)(2,1)S(1)}, bf16[15,1024]{1,0:T(8,128)(2,1)S(1)}, u32[]{:S(2)}, u32[]{:S(2)}) collective-permute-start(bf16[15,1024]{1,0:T(8,128)(2,1)S(1)} %get-tuple-element.59), channel_id=1, source_target_pairs={{0,1},{1,2},{2,3},{3,4},{4,5},{5,6},{6,7},{7,8},{8,9},{9,10},{10,1... | collective-permute-start | bytes 92168 | tf_op jit(solution)/shard_map/ppermute | solution.py:26
  255.3 38.4 %collective-permute-start.7 = (bf16[15,1024]{1,0:T(8,128)(2,1)S(1)}, bf16[15,1024]{1,0:T(8,128)(2,1)S(1)}, u32[]{:S(2)}, u32[]{:S(2)}) collective-permute-start(bf16[15,1024]{1,0:T(8,128)(2,1)S(1)} %get-tuple-element.60), channel_id=1, source_target_pairs={{1,0},{2,1},{3,2},{4,3},{5,4},{6,5},{7,6},{8,7},{9,8},{10,9},{11,1... | collective-permute-start | bytes 92168 | tf_op jit(solution)/shard_map/ppermute | solution.py:27
Sparse Core Ops, SparseCore 0:
  9.6 44.7 all-gather.10
  56.7 40.9 all-gather.8
  100.0 41.7 all-gather.6
  143.9 40.9 all-gather.12
  187.1 60.6 all-gather.14
  249.9 43.7 all-gather.16
where the time goes:
time: 310 us; the launch traced here: 309 us
  waiting for transfers between devices  207 us (67%)
  matrix products  43.7 us (14%)
  starting transfers between devices  22.5 us (7%)
  between operations  14.7 us (5%)
  other arithmetic  7.51 us (2%)
  local copies, waits for them, and re-layouts  7.22 us (2%)
  loops' own time  5.63 us (2%)
    all_gather x1, waiting for transfers between devices, shards(): glu_in = add_rows(norm_c, lax.all_gather(w_glu, 'tm', axis=0, tiled=True))  59.8 us
    all_gather x1, waiting for transfers between devices, shards(): key = add_rows(norm_a, lax.all_gather(w_key, 'tm', axis=0, tiled=True))  38.4 us
    all_gather x1, waiting for transfers between devices, shards(): value = add_rows(norm_a, lax.all_gather(w_value, 'tm', axis=0, tiled=True))  37.9 us
    all_gather x1, waiting for transfers between devices, shards(): lax.all_gather(w_proj, 'tm', axis=0, tiled=True)  35.1 us
    all_gather x1, waiting for transfers between devices, shards(): query = add_rows(norm_a, lax.all_gather(w_query, 'tm', axis=0, tiled=True))  28.6 us
    dot_general x6, matrix products, add_rows(): return jnp.dot(left, piece, preferred_element_type=jnp.float32)  23.8 us
    ppermute x6, starting transfers between devices, shifted(): return lax.ppermute(block, axis, route)  17.8 us
    dot_general x8, matrix products, one_head(): lax.dot_general(q_head, k_head, (((1,), (1,)), ((), ())), preferred_eleme...  10.8 us
  transfers between devices with their start and end apart: 14, of which 6 were waited for; matrix products, arithmetic and copies ran while one was open for 16% of the time, Pallas kernels for 0%

commit v1 on v0

--- a/solution.py
+++ b/solution.py
@@ -1,8 +1,11 @@
+import functools
 import math
 
 import jax
 import jax.numpy as jnp
 from jax import lax
+from jax.experimental import pallas as pl
+from jax.experimental.pallas import tpu as pltpu
 from jax.sharding import PartitionSpec as P
 
 HEADS = 8
@@ -75,7 +78,7 @@
     return jnp.transpose(stacked, (1, 0, 2)).reshape(width, HEADS * HEAD_DIM)
 
 
-def shards(
+def plain(
     frames,
     frame_count,
     lookback_mask,
@@ -129,9 +132,435 @@
     return (mid.astype(jnp.float32) + conv_sum).astype(jnp.bfloat16)
 
 
+F32 = jnp.float32
+BF16 = jnp.bfloat16
+MESH = pl.DeviceIdType.MESH
+TILE = 256
+
+
+def norm_rows(source, gain_ref, target):
+    rows = source.shape[0]
+
+    @pl.loop(0, rows // 32)
+    def _(step):
+        at = pl.ds(pl.multiple_of(step * 32, 32), 32)
+        xf = source[at, :].astype(F32)
+        mean = jnp.mean(xf, axis=-1, keepdims=True)
+        centered = xf - mean
+        var = jnp.mean(centered * centered, axis=-1, keepdims=True)
+        target[at, :] = (centered * lax.rsqrt(var + 1e-05) * gain_ref[...]).astype(BF16)
+
+
+def block(
+    n,
+    frames_ref, count_ref, look_ref, gain_a_ref, wq_ref, wk_ref, wv_ref, wo_ref, gain_c_ref,
+    wg_ref, taps_ref, scale_ref, shift_ref, wp_ref,
+    out_ref,
+    w_qkv, w_out, w_glu, w_proj, norm, counts, q_s, kv_s, ctx_s, mid_s, normc_s, gpad, act_s,
+    hsend, hrecv,
+    ring_send, ring_recv, x_send, x_recv, c_send, c_recv, n_send, n_recv, m_send, m_recv,
+    h_send, h_recv,
+):
+    g = lax.axis_index("groups")
+    t = lax.axis_index("tm")
+    core = lax.rem(t, 2)
+    chip = t // 2
+    chips = n // 2
+    deep = chips // 2
+    hops_a, hops_b = chips // 2, chips // 2 - 1
+    place = jnp.where(lax.rem(chip, 2) == 0, chip // 2, chips - 1 - chip // 2)
+    turn = 1 - 2 * core
+
+    def at_place(r):
+        r = lax.rem(r + 2 * chips, chips)
+        q = jnp.where(r < deep, 2 * r, 2 * (chips - 1 - r) + 1)
+        return 2 * q + core
+
+    next_a, next_b = at_place(place + turn), at_place(place - turn)
+    pair = t + turn
+    here = lambda index: (g, index)
+    across = (1 - g, t)
+
+    weights = (w_qkv, w_out, w_glu, w_proj)
+    depth = tuple(w.shape[0] // n for w in weights)
+    third = tuple(d // 48 * 16 for d in depth)
+
+    def rows(w, owner, start, size):
+        return weights[w].at[pl.ds(pl.multiple_of(owner * depth[w] + start, 16), size), :]
+
+    def copy(src, dst, send, recv, device):
+        return pltpu.make_async_remote_copy(
+            src_ref=src, dst_ref=dst, send_sem=send, recv_sem=recv,
+            device_id=device, device_id_type=MESH,
+        )
+
+    def ring(w, side, hop):
+        sign = turn if side == 0 else -turn
+        view = rows(w, at_place(place - sign * hop), g * third[w], depth[w] - third[w])
+        slot = hop + side * hops_a
+        target = next_a if side == 0 else next_b
+        return copy(view, view, ring_send.at[w, slot], ring_recv.at[w, slot], here(target))
+
+    def arrived(side, hop):
+        return at_place(place - (turn if side == 0 else -turn) * (hop + 1))
+
+    def over_x(w, side, hop):
+        view = rows(w, arrived(side, hop), g * (depth[w] - third[w]), third[w])
+        slot = hop + side * hops_a
+        return copy(view, view, x_send.at[w, slot], x_recv.at[w, slot], across)
+
+    def over_core(w, slot, owner):
+        view = rows(w, owner, 0, depth[w])
+        return copy(view, view, c_send.at[w, slot], c_recv.at[w, slot], here(pair))
+
+    sides = ((0, hops_a), (1, hops_b))
+
+    def begin(w):
+        ring(w, 0, 0).start()
+        ring(w, 1, 0).start()
+        over_core(w, chips - 1, t).start()
+
+    def step(w, hop):
+        for side, hops in sides:
+            if hop < hops:
+                ring(w, side, hop).wait_recv()
+                if hop + 1 < hops:
+                    ring(w, side, hop + 1).start()
+                over_x(w, side, hop).start()
+
+    def spread(w, hop):
+        for side, hops in sides:
+            if hop < hops:
+                over_x(w, side, hop).wait_recv()
+                over_core(w, hop + side * hops_a, arrived(side, hop)).start()
+
+    def ready(w):
+        for slot in range(chips):
+            over_core(w, slot, t).wait_recv()
+
+    barrier = pltpu.get_barrier_semaphore()
+    around = [lax.rem(t + n + d, n) for d in (1, -1, 2, -2)]
+    for device in [here(i) for i in (next_a, next_b, pair, *around)] + [across]:
+        pl.semaphore_signal(barrier, inc=1, device_id=device, device_id_type=MESH)
+
+    own = lambda w: pl.ds(pl.multiple_of(t * depth[w], 16), depth[w])
+    width = wq_ref.shape[1]
+    w_qkv[own(0), 0:width] = wq_ref[...]
+    w_qkv[own(0), width : 2 * width] = wk_ref[...]
+    w_qkv[own(0), 2 * width : 3 * width] = wv_ref[...]
+    w_out[own(1), :] = wo_ref[...]
+    w_glu[own(2), :] = wg_ref[...]
+    w_proj[own(3), :] = wp_ref[...]
+    pl.semaphore_wait(barrier, 8)
+    begin(0)
+    begin(1)
+
+    length = frames_ref.shape[0]
+    part = lambda i: norm.at[pl.ds(i * length, length), :]
+    norm_rows(frames_ref, gain_a_ref, part(2))
+    counts[2] = count_ref[...]
+    near = copy(part(2), part(1), n_send.at[0], n_recv.at[0], here(t + 1))
+    far = copy(part(2), part(0), n_send.at[1], n_recv.at[1], here(t + 2))
+    relay = copy(part(1), part(0), n_send.at[2], n_recv.at[1], here(t + 1))
+    near_count = copy(counts.at[2], counts.at[1], m_send.at[0], m_recv.at[0], here(t + 1))
+    far_count = copy(counts.at[2], counts.at[0], m_send.at[1], m_recv.at[1], here(t + 2))
+    even = core == 0
+
+    @pl.when(t + 1 < n)
+    def _():
+        near.start()
+        near_count.start()
+
+    @pl.when(t + 2 < n)
+    def _():
+        far_count.start()
+
+    @pl.when((t + 2 < n) & even)
+    def _():
+        far.start()
+
+    @pl.when(t < 2)
+    def _():
+        norm[0:length, :] = jnp.zeros((length, norm.shape[1]), BF16)
+        counts[0] = jnp.zeros(counts.shape[1:], jnp.int32)
+
+    @pl.when(t < 1)
+    def _():
+        norm[length : 2 * length, :] = jnp.zeros((length, norm.shape[1]), BF16)
+        counts[1] = jnp.zeros(counts.shape[1:], jnp.int32)
+
+    ctx_s[...] = jnp.zeros_like(ctx_s)
+
+    step(0, 0)
+    step(1, 0)
+
+    @pl.when(t >= 1)
+    def _():
+        near.wait_recv()
+        near_count.wait_recv()
+
+    @pl.when((t >= 1) & even)
+    def _():
+        relay.start()
+
+    for hop in range(1, hops_a):
+        step(0, hop)
+        spread(0, hop - 1)
+        step(1, hop)
+        spread(1, hop - 1)
+        if hop == hops_a - 2:
+            begin(2)
+            begin(3)
+    spread(0, hops_a - 1)
+
+    @pl.when(t >= 2)
+    def _():
+        far.wait_recv()
+        far_count.wait_recv()
+
+    ready(0)
+    spread(1, hops_a - 1)
+
+    @pl.loop(0, width // TILE)
+    def _(j):
+        cols = pl.ds(pl.multiple_of(j * TILE, TILE), TILE)
+        q_s[:, cols] = jnp.dot(
+            norm[2 * length : 3 * length, :], w_qkv[:, cols], preferred_element_type=F32
+        ).astype(BF16)
+
+    step(2, 0)
+    step(3, 0)
+
+    @pl.loop(0, 2 * width // TILE)
+    def _(j):
+        cols = pl.ds(pl.multiple_of(j * TILE, TILE), TILE)
+        source = pl.ds(pl.multiple_of(j * TILE + width, TILE), TILE)
+        kv_s[:, cols] = jnp.dot(norm[...], w_qkv[:, source], preferred_element_type=F32).astype(
+            BF16
+        )
+
+    step(2, 1)
+    step(3, 1)
+    spread(2, 0)
+    spread(3, 0)
+
+    lane = lax.broadcasted_iota(jnp.int32, (8, length), 1)
+    repeat = lambda v: jnp.concatenate([v] * (length // v.shape[1]), axis=1)
+    limits = [repeat(counts[i]) for i in range(3)]
+    seen = [
+        (lane < limits[0]) & (look_ref[:, 0:length] > 0),
+        (lane < limits[1]) & (look_ref[:, length : 2 * length] > 0),
+        lane < limits[2],
+    ]
+    hide = jnp.concatenate([jnp.where(s, 0.0, -1e30) for s in seen], axis=1)[0:1, :]
+    factor = math.log2(math.e) / math.sqrt(HEAD_DIM)
+
+    for head in range(HEADS):
+        first = head * HEAD_DIM
+        lo = first // 128 * 128
+        hi = -(-(first + HEAD_DIM) // 128) * 128
+        inside = lax.broadcasted_iota(jnp.int32, (length, hi - lo), 1) + lo
+        inside = (inside >= first) & (inside < first + HEAD_DIM)
+        q_head = jnp.where(inside, q_s[:, lo:hi].astype(F32), 0.0).astype(BF16)
+        scores = lax.dot_general(
+            q_head, kv_s[:, lo:hi], (((1,), (1,)), ((), ())), preferred_element_type=F32
+        )
+        scores = scores * factor + hide
+        top = jnp.max(scores, axis=1, keepdims=True)
+        expo = jnp.exp2(scores - top)
+        total = jnp.sum(expo, axis=1, keepdims=True)
+        context = jnp.dot(
+            expo.astype(BF16), kv_s[:, width + lo : width + hi], preferred_element_type=F32
+        )
+        context = context / total
+        ctx_s[:, lo:hi] = jnp.where(inside, context, ctx_s[:, lo:hi].astype(F32)).astype(BF16)
+        if head % 2 == 1 and head // 2 + 2 < hops_a:
+            hop = head // 2 + 2
+            step(2, hop)
+            spread(2, hop - 1)
+            step(3, hop)
+            spread(3, hop - 1)
+    for hop in range(HEADS // 2 + 2, hops_a):
+        step(2, hop)
+        spread(2, hop - 1)
+        step(3, hop)
+        spread(3, hop - 1)
+    ready(1)
+
+    @pl.loop(0, mid_s.shape[1] // TILE)
+    def _(j):
+        cols = pl.ds(pl.multiple_of(j * TILE, TILE), TILE)
+        add = jnp.dot(ctx_s[...], w_out[:, cols], preferred_element_type=F32)
+        mid_s[:, cols] = (frames_ref[:, cols].astype(F32) + add).astype(BF16)
+
+    spread(2, hops_a - 1)
+    norm_rows(mid_s, gain_c_ref, normc_s)
+    spread(3, hops_a - 1)
+    ready(2)
+
+    half_width = w_glu.shape[1] // 2
+    live = lax.broadcasted_iota(jnp.int32, (length, 1), 0) < count_ref[0:1, 0:1]
+
+    @pl.loop(0, half_width // TILE)
+    def _(j):
+        cols = pl.ds(pl.multiple_of(j * TILE, TILE), TILE)
+        gate_cols = pl.ds(pl.multiple_of(j * TILE + half_width, TILE), TILE)
+        left = jnp.dot(normc_s[...], w_glu[:, cols], preferred_element_type=F32)
+        gate = jnp.dot(normc_s[...], w_glu[:, gate_cols], preferred_element_type=F32)
+        gated = jnp.where(live, left * jax.nn.sigmoid(gate), 0.0).astype(BF16)
+        gpad[16 : 16 + length, cols] = gated.astype(F32)
+        hsend[0, :, cols] = gated[0:16]
+        hsend[1, :, cols] = gated[length - 16 : length]
+
+    below = copy(hsend.at[1], hrecv.at[0], h_send.at[0], h_recv.at[0], here(t + 1))
+    above = copy(hsend.at[0], hrecv.at[1], h_send.at[1], h_recv.at[1], here(t - 1))
+
+    @pl.when(t + 1 < n)
+    def _():
+        below.start()
+
+    @pl.when(t >= 1)
+    def _():
+        above.start()
+
+    @pl.when(t >= 1)
+    def _():
+        below.wait_recv()
+        gpad[0:16, :] = hrecv[0].astype(F32)
+
+    @pl.when(t < 1)
+    def _():
+        gpad[0:16, :] = jnp.zeros((16, half_width), F32)
+
+    @pl.when(t + 1 < n)
+    def _():
+        above.wait_recv()
+        gpad[16 + length : 32 + length, :] = hrecv[1].astype(F32)
+
+    @pl.when(t + 1 >= n)
+    def _():
+        gpad[16 + length : 32 + length, :] = jnp.zeros((16, half_width), F32)
+
+    strip = 128
+
+    @pl.loop(0, half_width // 128)
+    def _(j):
+        cols = pl.ds(pl.multiple_of(j * 128, 128), 128)
+        for start in range(0, length, strip):
+            conv = jnp.zeros((strip, 128), F32)
+            for shift in range(8):
+                moved = gpad[start + shift : start + shift + strip + 24, cols]
+                for at in range(shift, 32, 8):
+                    if at >= 1:
+                        conv = conv + taps_ref[at - 1 : at, cols] * moved[at - shift : at - shift + strip]
+            pre = conv * scale_ref[:, cols] + shift_ref[:, cols]
+            act_s[start : start + strip, cols] = (pre * jax.nn.sigmoid(pre)).astype(BF16)
+
+    ready(3)
+
+    @pl.loop(0, out_ref.shape[1] // TILE)
+    def _(j):
+        cols = pl.ds(pl.multiple_of(j * TILE, TILE), TILE)
+        add = jnp.dot(act_s[...], w_proj[:, cols], preferred_element_type=F32)
+        out_ref[:, cols] = (mid_s[:, cols].astype(F32) + add).astype(BF16)
+
+    for w in range(4):
+        for side, hops in sides:
+            for hop in range(hops):
+                ring(w, side, hop).wait_send()
+                over_x(w, side, hop).wait_send()
+        for slot in range(chips):
+            over_core(w, slot, t).wait_send()
+
+    @pl.when(t + 1 < n)
+    def _():
+        near.wait_send()
+        near_count.wait_send()
+        below.wait_send()
+
+    @pl.when(t >= 1)
+    def _():
+        above.wait_send()
+
+    @pl.when(t + 2 < n)
+    def _():
+        far_count.wait_send()
+
+    @pl.when((t + 2 < n) & even)
+    def _():
+        far.wait_send()
+
+    @pl.when((t >= 1) & even)
+    def _():
+        relay.wait_send()
+
+
+def fused(
+    n, frames, frame_count, lookback_mask, attn_gain, w_query, w_key, w_value, w_out, conv_gain,
+    w_glu, depthwise, conv_scale, conv_shift, w_proj,
+):
+    length, model = frames.shape
+    width = w_query.shape[1]
+    half = w_glu.shape[1] // 2
+    chips = n // 2
+    count = jnp.broadcast_to(frame_count.reshape(1, 1), (8, 128))
+    look = jnp.broadcast_to(jnp.repeat(lookback_mask, length // 2, axis=1), (8, 2 * length))
+    dma = pltpu.SemaphoreType.DMA
+    params = 3 * width * model + model * width + 2 * half * model + half * model
+    return pl.pallas_call(
+        functools.partial(block, n),
+        out_shape=jax.ShapeDtypeStruct((length, model), BF16),
+        in_specs=[pl.BlockSpec(memory_space=pltpu.VMEM)] * 14,
+        out_specs=pl.BlockSpec(memory_space=pltpu.VMEM),
+        scratch_shapes=[
+            pltpu.VMEM((model, 3 * width), BF16),
+            pltpu.VMEM((width, model), BF16),
+            pltpu.VMEM((model, 2 * half), BF16),
+            pltpu.VMEM((half, model), BF16),
+            pltpu.VMEM((3 * length, model), BF16),
+            pltpu.VMEM((3, 8, 128), jnp.int32),
+            pltpu.VMEM((length, width), BF16),
+            pltpu.VMEM((3 * length, 2 * width), BF16),
+            pltpu.VMEM((length, width), BF16),
+            pltpu.VMEM((length, model), BF16),
+            pltpu.VMEM((length, model), BF16),
+            pltpu.VMEM((length + 32, half), F32),
+            pltpu.VMEM((length, half), BF16),
+            pltpu.VMEM((2, 16, half), BF16),
+            pltpu.VMEM((2, 16, half), BF16),
+            dma((4, chips - 1)), dma((4, chips - 1)),
+            dma((4, chips - 1)), dma((4, chips - 1)),
+            dma((4, chips)), dma((4, chips)),
+            dma((3,)), dma((2,)), dma((2,)), dma((2,)), dma((2,)), dma((2,)),
+        ],
+        compiler_params=pltpu.CompilerParams(
+            collective_id=0, has_side_effects=True, vmem_limit_bytes=56 * 1024 * 1024
+        ),
+        cost_estimate=pl.CostEstimate(
+            flops=2 * length * params, bytes_accessed=2 * params, transcendentals=length * half
+        ),
+    )(
+        frames, count, look, attn_gain.reshape(1, -1), w_query, w_key, w_value, w_out,
+        conv_gain.reshape(1, -1), w_glu, depthwise, conv_scale.reshape(1, -1),
+        conv_shift.reshape(1, -1), w_proj,
+    )
+
+
+def shards(groups, *args):
+    n = lax.axis_size("tm")
+    frames, w_query, w_out, w_glu, w_proj = args[0], args[4], args[7], args[9], args[13]
+    whole = all(w.shape[0] % 16 == 0 and w.shape[0] >= 48 for w in (w_query, w_out, w_glu, w_proj))
+    tiles = all(
+        w.shape[1] % TILE == 0 for w in (w_query, w_out, w_proj)
+    ) and w_glu.shape[1] % (2 * TILE) == 0
+    if groups == 2 and n % 8 == 0 and whole and tiles and frames.shape[0] % 256 == 0:
+        return fused(n, *args)
+    return plain(*args)
+
+
 def solution(mesh):
     return jax.shard_map(
-        shards,
+        functools.partial(shards, mesh.shape["groups"]),
         mesh=mesh,
         in_specs=(
             P(("groups", "tm"), None),

time: 310 us -> 116 us (0.37)
  waiting for transfers between devices: 207 us -> 0 us
  Pallas kernels: 0 us -> 111 us
  matrix products: 43.7 us -> 0 us
  starting transfers between devices: 22.5 us -> 0 us
  between operations: 14.7 us -> 0.69 us
  other arithmetic: 7.51 us -> 0 us
  loops' own time: 5.63 us -> 0 us
    all_gather x6 -> x0, waiting for transfers between devices: 204 us -> none  [the longest x1 59.8 us: shards(): glu_in = add_rows(norm_c, lax.all_gather(w_glu, 'tm', axis=0, tiled=True))]
    pallas_call x0 -> x1, Pallas kernels: none -> 111 us  [fused(): pl.pallas_call(functools.partial(block, n), out_shape=jax.ShapeDtypeStruc...]
    dot_general x22 -> x0, matrix products: 43.7 us -> none  [the longest x6 23.8 us: add_rows(): return jnp.dot(left, piece, preferred_element_type=jnp.float32)]
    ppermute x8 -> x0, starting transfers between devices: 22.3 us -> none  [the longest x6 17.8 us: shifted(): return lax.ppermute(block, axis, route)]
    another operation x1 -> x0, loops' own time: 5.63 us -> none  [attend(): stacked = lax.map(one_head, jnp.arange(HEADS, dtype=jnp.int32))]
    dynamic_slice x8 -> x0, local copies, waits for them, and re-layouts: 5.3 us -> none  [attend(): stacked = lax.map(one_head, jnp.arange(HEADS, dtype=jnp.int32))]
    unnamed x6 -> x0, waiting for transfers between devices: 3.16 us -> none
    reduce_sum x12 -> x0, other arithmetic: 3.14 us -> none  [the longest x8 2.23 us: one_head(): weights = (expo / jnp.sum(expo, axis=1, keepdims=True)).astype(jnp.bfloat16)]
  transfers between devices with their start and end apart: 14 -> 0, of which waited for: 6 -> 0; matrix products, arithmetic and copies ran while one was open for 16% -> 0% of each run, Pallas kernels for 0% -> 0%
where the time goes in v1:
time: 116 us
  Pallas kernels  111 us (96%)
  local copies, waits for them, and re-layouts  4.63 us (4%)
    pallas_call x1, Pallas kernels, fused(): pl.pallas_call(functools.partial(block, n), out_shape=jax.ShapeDtypeStruc...  111 us

profile of v1, /device:TPU:1, one launch (start us, length us, event | category | flops | bytes accessed | tf_op | source)
XLA Modules:
  0.0 116.0 jit_solution(17107541494178372095)
XLA Ops:
  0.0 0.0 copy-start
  0.0 0.0 copy-start.1
  0.7 0.0 copy-done
  0.7 0.1 broadcast_bitcast_fusion
  0.8 0.6 broadcast_in_dim.18.count_ref
  1.3 0.0 copy-done.1
  1.3 0.0 copy-start.2
  1.4 0.6 reshape.19.gain_a_ref
  1.9 0.1 copy-done.2
  2.1 0.6 reshape.20.gain_c_ref
  2.6 0.6 broadcast_in_dim.21.look_ref
  3.2 110.7 %shard_map.139 = bf16[256,1536]{1,0:T(8,128)(2,1)} custom-call(bf16[256,1536]{1,0:T(8,128)(2,1)} %frames_ref.1, s32[8,128]{1,0:T(8,128)} %broadcast_in_dim.18.count_ref, s32[8,512]{1,0:T(8,128)} %broadcast_in_dim.21.look_ref, f32[1,1536]{1,0:T(1,128)} %reshape.19.gain_a_ref, bf16[96,768]{1,0:T(8,128)(2,1)} %wq_ref.1, bf16[96,768]{1,0:T(8,128)(2,1)} %wk_ref.1, ...), custom_call_target="tpu_custom_call" | custom-call | flops 4831838208 | bytes 18874368 | tf_op jit(solution)/shard_map/pallas_call | solution.py:510
  114.0 2.1 %copy.17 = bf16[256,1536]{1,0:T(8,128)(2,1)} copy(bf16[256,1536]{1,0:T(8,128)(2,1)} %shard_map.139) | data formatting | bytes 1572864
Async XLA Ops:
  0.0 0.7 copy-start
  0.0 1.3 %copy-start.1 = (f32[1536]{0:T(1024)S(1)}, f32[1536]{0:T(1024)}, u32[]{:S(2)}) copy-start(f32[1536]{0:T(1024)} %param.17) | copy-start | bytes 18436
  1.3 0.7 copy-start.2

commit v2 on v1

--- a/solution.py
+++ b/solution.py
@@ -148,7 +148,7 @@
         mean = jnp.mean(xf, axis=-1, keepdims=True)
         centered = xf - mean
         var = jnp.mean(centered * centered, axis=-1, keepdims=True)
-        target[at, :] = (centered * lax.rsqrt(var + 1e-05) * gain_ref[...]).astype(BF16)
+        target[at, :] = (centered * lax.rsqrt(var + 1e-05) * gain_ref[...].reshape(1, -1)).astype(BF16)
 
 
 def block(
@@ -183,10 +183,23 @@
 
     weights = (w_qkv, w_out, w_glu, w_proj)
     depth = tuple(w.shape[0] // n for w in weights)
-    third = tuple(d // 48 * 16 for d in depth)
-
-    def rows(w, owner, start, size):
-        return weights[w].at[pl.ds(pl.multiple_of(owner * depth[w] + start, 16), size), :]
+    full = tuple(w.shape[1] for w in weights)
+    around_cols = tuple((61 * c + 6400) // 12800 * 128 for c in full)
+    pieces = tuple(
+        (w, start, size)
+        for w, parts in enumerate((2, 1, 2, 1))
+        for size in [depth[w] // parts if depth[w] % (16 * parts) == 0 else depth[w]]
+        for start in range(0, depth[w], size)
+    )
+
+    def rows(p, owner, start, size):
+        w, low, high = pieces[p]
+        at = pl.ds(pl.multiple_of(owner * depth[w] + low, 16), high)
+        return weights[w].at[at, pl.ds(pl.multiple_of(start, 128), size)]
+
+    def sizes(p):
+        w = pieces[p][0]
+        return full[w], around_cols[w]
 
     def copy(src, dst, send, recv, device):
         return pltpu.make_async_remote_copy(
@@ -196,7 +209,8 @@
 
     def ring(w, side, hop):
         sign = turn if side == 0 else -turn
-        view = rows(w, at_place(place - sign * hop), g * third[w], depth[w] - third[w])
+        cols, ringed = sizes(w)
+        view = rows(w, at_place(place - sign * hop), g * (cols - ringed), ringed)
         slot = hop + side * hops_a
         target = next_a if side == 0 else next_b
         return copy(view, view, ring_send.at[w, slot], ring_recv.at[w, slot], here(target))
@@ -205,12 +219,13 @@
         return at_place(place - (turn if side == 0 else -turn) * (hop + 1))
 
     def over_x(w, side, hop):
-        view = rows(w, arrived(side, hop), g * (depth[w] - third[w]), third[w])
+        cols, ringed = sizes(w)
+        view = rows(w, arrived(side, hop), g * ringed, cols - ringed)
         slot = hop + side * hops_a
         return copy(view, view, x_send.at[w, slot], x_recv.at[w, slot], across)
 
     def over_core(w, slot, owner):
-        view = rows(w, owner, 0, depth[w])
+        view = rows(w, owner, 0, sizes(w)[0])
         return copy(view, view, c_send.at[w, slot], c_recv.at[w, slot], here(pair))
 
     sides = ((0, hops_a), (1, hops_b))
@@ -220,7 +235,10 @@
         ring(w, 1, 0).start()
         over_core(w, chips - 1, t).start()
 
+    stepped, spreaded, rounds = set(), set(), []
+
     def step(w, hop):
+        stepped.add((w, hop))
         for side, hops in sides:
             if hop < hops:
                 ring(w, side, hop).wait_recv()
@@ -229,14 +247,43 @@
                 over_x(w, side, hop).start()
 
     def spread(w, hop):
+        if (w, hop) in spreaded:
+            return
+        spreaded.add((w, hop))
         for side, hops in sides:
             if hop < hops:
                 over_x(w, side, hop).wait_recv()
                 over_core(w, hop + side * hops_a, arrived(side, hop)).start()
 
+    turns = (0, 0, 2, 3, 4, 5)
+
+    def advance():
+        number = len(rounds)
+        rounds.append(number)
+        for p, first in enumerate(turns):
+            hop = number - first - 1
+            if hop == -1:
+                begin(p)
+            if 0 <= hop < hops_a:
+                step(p, hop)
+            if 0 < hop <= hops_a:
+                spread(p, hop - 1)
+
+    def finish(w):
+        for p, piece in enumerate(pieces):
+            if piece[0] == w:
+                while (p, hops_a - 1) not in stepped:
+                    advance()
+        for p, piece in enumerate(pieces):
+            if piece[0] == w:
+                spread(p, hops_a - 1)
+
     def ready(w):
-        for slot in range(chips):
-            over_core(w, slot, t).wait_recv()
+        finish(w)
+        for p, piece in enumerate(pieces):
+            if piece[0] == w:
+                for slot in range(chips):
+                    over_core(p, slot, t).wait_recv()
 
     barrier = pltpu.get_barrier_semaphore()
     around = [lax.rem(t + n + d, n) for d in (1, -1, 2, -2)]
@@ -252,13 +299,12 @@
     w_glu[own(2), :] = wg_ref[...]
     w_proj[own(3), :] = wp_ref[...]
     pl.semaphore_wait(barrier, 8)
-    begin(0)
-    begin(1)
+    advance()
 
     length = frames_ref.shape[0]
     part = lambda i: norm.at[pl.ds(i * length, length), :]
     norm_rows(frames_ref, gain_a_ref, part(2))
-    counts[2] = count_ref[...]
+    counts[2] = jnp.full(counts.shape[1:], count_ref[0], jnp.int32)
     near = copy(part(2), part(1), n_send.at[0], n_recv.at[0], here(t + 1))
     far = copy(part(2), part(0), n_send.at[1], n_recv.at[1], here(t + 2))
     relay = copy(part(1), part(0), n_send.at[2], n_recv.at[1], here(t + 1))
@@ -291,8 +337,7 @@
 
     ctx_s[...] = jnp.zeros_like(ctx_s)
 
-    step(0, 0)
-    step(1, 0)
+    advance()
 
     @pl.when(t >= 1)
     def _():
@@ -303,15 +348,7 @@
     def _():
         relay.start()
 
-    for hop in range(1, hops_a):
-        step(0, hop)
-        spread(0, hop - 1)
-        step(1, hop)
-        spread(1, hop - 1)
-        if hop == hops_a - 2:
-            begin(2)
-            begin(3)
-    spread(0, hops_a - 1)
+    finish(0)
 
     @pl.when(t >= 2)
     def _():
@@ -319,7 +356,6 @@
         far_count.wait_recv()
 
     ready(0)
-    spread(1, hops_a - 1)
 
     @pl.loop(0, width // TILE)
     def _(j):
@@ -328,31 +364,28 @@
             norm[2 * length : 3 * length, :], w_qkv[:, cols], preferred_element_type=F32
         ).astype(BF16)
 
-    step(2, 0)
-    step(3, 0)
-
-    @pl.loop(0, 2 * width // TILE)
-    def _(j):
-        cols = pl.ds(pl.multiple_of(j * TILE, TILE), TILE)
-        source = pl.ds(pl.multiple_of(j * TILE + width, TILE), TILE)
-        kv_s[:, cols] = jnp.dot(norm[...], w_qkv[:, source], preferred_element_type=F32).astype(
-            BF16
-        )
-
-    step(2, 1)
-    step(3, 1)
-    spread(2, 0)
-    spread(3, 0)
-
-    lane = lax.broadcasted_iota(jnp.int32, (8, length), 1)
-    repeat = lambda v: jnp.concatenate([v] * (length // v.shape[1]), axis=1)
-    limits = [repeat(counts[i]) for i in range(3)]
-    seen = [
-        (lane < limits[0]) & (look_ref[:, 0:length] > 0),
-        (lane < limits[1]) & (look_ref[:, length : 2 * length] > 0),
-        lane < limits[2],
-    ]
-    hide = jnp.concatenate([jnp.where(s, 0.0, -1e30) for s in seen], axis=1)[0:1, :]
+    def spans(base):
+        @pl.loop(0, width // TILE)
+        def _(j):
+            cols = pl.ds(pl.multiple_of(base + j * TILE, TILE), TILE)
+            source = pl.ds(pl.multiple_of(base + width + j * TILE, TILE), TILE)
+            kv_s[:, cols] = jnp.dot(
+                norm[...], w_qkv[:, source], preferred_element_type=F32
+            ).astype(BF16)
+
+    spans(0)
+    advance()
+    spans(width)
+
+    lane = lax.broadcasted_iota(jnp.int32, (1, 128), 1)
+    hide = []
+    for b in range(3 * length // 128):
+        limit = counts[b * 128 // length][0:1, :] - b * 128 % length
+        seen = lane < limit
+        if b * 128 < 2 * length:
+            seen = seen & (jnp.full((1, 128), look_ref[0, b * 128 // (length // 2)], jnp.int32) > 0)
+        hide.append(jnp.where(seen, 0.0, -1e30))
+    hide = jnp.concatenate(hide, axis=1)
     factor = math.log2(math.e) / math.sqrt(HEAD_DIM)
 
     for head in range(HEADS):
@@ -374,17 +407,10 @@
         )
         context = context / total
         ctx_s[:, lo:hi] = jnp.where(inside, context, ctx_s[:, lo:hi].astype(F32)).astype(BF16)
-        if head % 2 == 1 and head // 2 + 2 < hops_a:
-            hop = head // 2 + 2
-            step(2, hop)
-            spread(2, hop - 1)
-            step(3, hop)
-            spread(3, hop - 1)
-    for hop in range(HEADS // 2 + 2, hops_a):
-        step(2, hop)
-        spread(2, hop - 1)
-        step(3, hop)
-        spread(3, hop - 1)
+        if head == 1:
+            advance()
+        if head == 6:
+            advance()
     ready(1)
 
     @pl.loop(0, mid_s.shape[1] // TILE)
@@ -393,13 +419,11 @@
         add = jnp.dot(ctx_s[...], w_out[:, cols], preferred_element_type=F32)
         mid_s[:, cols] = (frames_ref[:, cols].astype(F32) + add).astype(BF16)
 
-    spread(2, hops_a - 1)
     norm_rows(mid_s, gain_c_ref, normc_s)
-    spread(3, hops_a - 1)
     ready(2)
 
     half_width = w_glu.shape[1] // 2
-    live = lax.broadcasted_iota(jnp.int32, (length, 1), 0) < count_ref[0:1, 0:1]
+    live = lax.broadcasted_iota(jnp.int32, (length, 1), 0) < count_ref[0]
 
     @pl.loop(0, half_width // TILE)
     def _(j):
@@ -423,6 +447,8 @@
     def _():
         above.start()
 
+    advance()
+
     @pl.when(t >= 1)
     def _():
         below.wait_recv()
@@ -441,6 +467,7 @@
     def _():
         gpad[16 + length : 32 + length, :] = jnp.zeros((16, half_width), F32)
 
+    finish(3)
     strip = 128
 
     @pl.loop(0, half_width // 128)
@@ -464,7 +491,7 @@
         add = jnp.dot(act_s[...], w_proj[:, cols], preferred_element_type=F32)
         out_ref[:, cols] = (mid_s[:, cols].astype(F32) + add).astype(BF16)
 
-    for w in range(4):
+    for w in range(len(pieces)):
         for side, hops in sides:
             for hop in range(hops):
                 ring(w, side, hop).wait_send()
@@ -503,14 +530,13 @@
     width = w_query.shape[1]
     half = w_glu.shape[1] // 2
     chips = n // 2
-    count = jnp.broadcast_to(frame_count.reshape(1, 1), (8, 128))
-    look = jnp.broadcast_to(jnp.repeat(lookback_mask, length // 2, axis=1), (8, 2 * length))
+    inside, scalars = (pl.BlockSpec(memory_space=m) for m in (pltpu.VMEM, pltpu.SMEM))
     dma = pltpu.SemaphoreType.DMA
     params = 3 * width * model + model * width + 2 * half * model + half * model
     return pl.pallas_call(
         functools.partial(block, n),
         out_shape=jax.ShapeDtypeStruct((length, model), BF16),
-        in_specs=[pl.BlockSpec(memory_space=pltpu.VMEM)] * 14,
+        in_specs=[inside, scalars, scalars] + [inside] * 11,
         out_specs=pl.BlockSpec(memory_space=pltpu.VMEM),
         scratch_shapes=[
             pltpu.VMEM((model, 3 * width), BF16),
@@ -528,9 +554,9 @@
             pltpu.VMEM((length, half), BF16),
             pltpu.VMEM((2, 16, half), BF16),
             pltpu.VMEM((2, 16, half), BF16),
-            dma((4, chips - 1)), dma((4, chips - 1)),
-            dma((4, chips - 1)), dma((4, chips - 1)),
-            dma((4, chips)), dma((4, chips)),
+            dma((6, chips - 1)), dma((6, chips - 1)),
+            dma((6, chips - 1)), dma((6, chips - 1)),
+            dma((6, chips)), dma((6, chips)),
             dma((3,)), dma((2,)), dma((2,)), dma((2,)), dma((2,)), dma((2,)),
         ],
         compiler_params=pltpu.CompilerParams(
@@ -540,8 +566,8 @@
             flops=2 * length * params, bytes_accessed=2 * params, transcendentals=length * half
         ),
     )(
-        frames, count, look, attn_gain.reshape(1, -1), w_query, w_key, w_value, w_out,
-        conv_gain.reshape(1, -1), w_glu, depthwise, conv_scale.reshape(1, -1),
+        frames, frame_count, lookback_mask, attn_gain, w_query, w_key, w_value, w_out,
+        conv_gain, w_glu, depthwise, conv_scale.reshape(1, -1),
         conv_shift.reshape(1, -1), w_proj,
     )
 

time: 116 us -> 114 us (0.983)
  local copies, waits for them, and re-layouts: 4.63 us -> 2.06 us
    broadcast_in_dim x3 -> x0, local copies, waits for them, and re-layouts: 1.27 us -> none  [the longest x1 0.61 us: fused(): jnp.broadcast_to(jnp.repeat(lookback_mask, length // 2, axis=1), (8, 2 *...]
    reshape x2 -> x0, local copies, waits for them, and re-layouts: 1.18 us -> none  [the longest x1 0.59 us: fused(): attn_gain.reshape(1, -1)]
where the time goes in v2:
time: 114 us
  Pallas kernels  111 us (97%)
  local copies, waits for them, and re-layouts  2.06 us (2%)
    pallas_call x1, Pallas kernels, fused(): pl.pallas_call(functools.partial(block, n), out_shape=jax.ShapeDtypeStruc...  111 us

profile of v2, /device:TPU:1, one launch (start us, length us, event | category | flops | bytes accessed | tf_op | source)
XLA Modules:
  0.0 113.7 jit_solution(1215411084634507670)
XLA Ops:
  0.7 111.0 %shard_map.136 = bf16[256,1536]{1,0:T(8,128)(2,1)} custom-call(bf16[256,1536]{1,0:T(8,128)(2,1)} %frames_ref.1, s32[1]{0:T(128)S(6)} %copy.16.count_ref, s32[1,4]{1,0:T(1,128)} %look_ref.1, f32[1536]{0:T(1024)} %gain_a_ref.1, bf16[96,768]{1,0:T(8,128)(2,1)} %wq_ref.1, bf16[96,768]{1,0:T(8,128)(2,1)} %wk_ref.1, bf16[96,768]{1,0:T(8,128)(2,1)} %wv_ref.1, ...), custom_call_target="tpu_custom_call" | custom-call | flops 4831838208 | bytes 18874368 | tf_op jit(solution)/shard_map/pallas_call | solution.py:536
  111.6 2.1 %copy.17 = bf16[256,1536]{1,0:T(8,128)(2,1)} copy(bf16[256,1536]{1,0:T(8,128)(2,1)} %shard_map.136) | data formatting | bytes 1572864

commit v3 on v2

--- a/solution.py
+++ b/solution.py
@@ -156,7 +156,7 @@
     frames_ref, count_ref, look_ref, gain_a_ref, wq_ref, wk_ref, wv_ref, wo_ref, gain_c_ref,
     wg_ref, taps_ref, scale_ref, shift_ref, wp_ref,
     out_ref,
-    w_qkv, w_out, w_glu, w_proj, norm, counts, q_s, kv_s, ctx_s, mid_s, normc_s, gpad, act_s,
+    w_qkv, w_out, w_glu, w_proj, norm, counts, hide_s, qt_s, k_s, vt_s, ctxt_s, ctx_s, mid_s, normc_s, gpad, act_s,
     hsend, hrecv,
     ring_send, ring_recv, x_send, x_recv, c_send, c_recv, n_send, n_recv, m_send, m_recv,
     h_send, h_recv,
@@ -183,23 +183,26 @@
 
     weights = (w_qkv, w_out, w_glu, w_proj)
     depth = tuple(w.shape[0] // n for w in weights)
-    full = tuple(w.shape[1] for w in weights)
-    around_cols = tuple((61 * c + 6400) // 12800 * 128 for c in full)
-    pieces = tuple(
-        (w, start, size)
-        for w, parts in enumerate((2, 1, 2, 1))
-        for size in [depth[w] // parts if depth[w] % (16 * parts) == 0 else depth[w]]
-        for start in range(0, depth[w], size)
-    )
+    width = wq_ref.shape[1]
+    halves = depth[2] // 2 if depth[2] % 32 == 0 else depth[2]
+    pieces = [
+        (0, 0, depth[0], width, width, 61),
+        (0, 0, depth[0], 2 * width, width, 50),
+        (0, 0, depth[0], 0, width, 50),
+        (1, 0, depth[1], 0, w_out.shape[1], 61),
+        (2, 0, halves, 0, w_glu.shape[1], 61),
+        (2, depth[2] - halves, halves, 0, w_glu.shape[1], 61),
+        (3, 0, depth[3], 0, w_proj.shape[1], 61),
+    ]
 
     def rows(p, owner, start, size):
-        w, low, high = pieces[p]
+        w, low, high, first = pieces[p][:4]
         at = pl.ds(pl.multiple_of(owner * depth[w] + low, 16), high)
-        return weights[w].at[at, pl.ds(pl.multiple_of(start, 128), size)]
+        return weights[w].at[at, pl.ds(pl.multiple_of(first + start, 128), size)]
 
     def sizes(p):
-        w = pieces[p][0]
-        return full[w], around_cols[w]
+        cols, share = pieces[p][4:]
+        return cols, (share * cols + 6400) // 12800 * 128
 
     def copy(src, dst, send, recv, device):
         return pltpu.make_async_remote_copy(
@@ -255,7 +258,7 @@
                 over_x(w, side, hop).wait_recv()
                 over_core(w, hop + side * hops_a, arrived(side, hop)).start()
 
-    turns = (0, 0, 2, 3, 4, 5)
+    turns = (0, 0, 1, 3, 4, 4, 5)
 
     def advance():
         number = len(rounds)
@@ -269,21 +272,18 @@
             if 0 < hop <= hops_a:
                 spread(p, hop - 1)
 
-    def finish(w):
-        for p, piece in enumerate(pieces):
-            if piece[0] == w:
-                while (p, hops_a - 1) not in stepped:
-                    advance()
-        for p, piece in enumerate(pieces):
-            if piece[0] == w:
-                spread(p, hops_a - 1)
-
-    def ready(w):
-        finish(w)
-        for p, piece in enumerate(pieces):
-            if piece[0] == w:
-                for slot in range(chips):
-                    over_core(p, slot, t).wait_recv()
+    def finish(*which):
+        for p in which:
+            while (p, hops_a - 1) not in stepped:
+                advance()
+        for p in which:
+            spread(p, hops_a - 1)
+
+    def ready(*which):
+        finish(*which)
+        for p in which:
+            for slot in range(chips):
+                over_core(p, slot, t).wait_recv()
 
     barrier = pltpu.get_barrier_semaphore()
     around = [lax.rem(t + n + d, n) for d in (1, -1, 2, -2)]
@@ -291,7 +291,6 @@
         pl.semaphore_signal(barrier, inc=1, device_id=device, device_id_type=MESH)
 
     own = lambda w: pl.ds(pl.multiple_of(t * depth[w], 16), depth[w])
-    width = wq_ref.shape[1]
     w_qkv[own(0), 0:width] = wq_ref[...]
     w_qkv[own(0), width : 2 * width] = wk_ref[...]
     w_qkv[own(0), 2 * width : 3 * width] = wv_ref[...]
@@ -335,8 +334,6 @@
         norm[length : 2 * length, :] = jnp.zeros((length, norm.shape[1]), BF16)
         counts[1] = jnp.zeros(counts.shape[1:], jnp.int32)
 
-    ctx_s[...] = jnp.zeros_like(ctx_s)
-
     advance()
 
     @pl.when(t >= 1)
@@ -355,63 +352,68 @@
         far.wait_recv()
         far_count.wait_recv()
 
-    ready(0)
-
-    @pl.loop(0, width // TILE)
-    def _(j):
-        cols = pl.ds(pl.multiple_of(j * TILE, TILE), TILE)
-        q_s[:, cols] = jnp.dot(
-            norm[2 * length : 3 * length, :], w_qkv[:, cols], preferred_element_type=F32
-        ).astype(BF16)
-
-    def spans(base):
-        @pl.loop(0, width // TILE)
-        def _(j):
-            cols = pl.ds(pl.multiple_of(base + j * TILE, TILE), TILE)
-            source = pl.ds(pl.multiple_of(base + width + j * TILE, TILE), TILE)
-            kv_s[:, cols] = jnp.dot(
-                norm[...], w_qkv[:, source], preferred_element_type=F32
-            ).astype(BF16)
-
-    spans(0)
-    advance()
-    spans(width)
-
-    lane = lax.broadcasted_iota(jnp.int32, (1, 128), 1)
-    hide = []
+    across_rows = lax.broadcasted_iota(jnp.int32, (128, 128), 0)
     for b in range(3 * length // 128):
         limit = counts[b * 128 // length][0:1, :] - b * 128 % length
-        seen = lane < limit
+        seen = across_rows < limit
         if b * 128 < 2 * length:
-            seen = seen & (jnp.full((1, 128), look_ref[0, b * 128 // (length // 2)], jnp.int32) > 0)
-        hide.append(jnp.where(seen, 0.0, -1e30))
-    hide = jnp.concatenate(hide, axis=1)
+            allowed = look_ref[0, b * 128 // (length // 2)]
+            seen = seen & (jnp.full((128, 128), allowed, jnp.int32) > 0)
+        hide_s[b * 128 : (b + 1) * 128, :] = jnp.where(seen, 0.0, -1e30)
+
+    def tiles(size):
+        return lambda body: pl.loop(0, size // TILE)(
+            lambda j: body(lambda base: pl.ds(pl.multiple_of(base + j * TILE, TILE), TILE))
+        )
+
+    ready(0)
+
+    @tiles(width)
+    def _(at):
+        k_s[:, at(0)] = jnp.dot(
+            norm[...], w_qkv[:, at(width)], preferred_element_type=F32
+        ).astype(BF16)
+
+    ready(1)
+
+    @tiles(width)
+    def _(at):
+        value = jnp.dot(norm[...], w_qkv[:, at(2 * width)], preferred_element_type=F32)
+        vt_s[at(0), :] = value.T.astype(BF16)
+
+    ready(2)
+
+    @tiles(width)
+    def _(at):
+        query = jnp.dot(norm[2 * length :, :], w_qkv[:, at(0)], preferred_element_type=F32)
+        qt_s[at(0), :] = query.T.astype(BF16)
+
     factor = math.log2(math.e) / math.sqrt(HEAD_DIM)
-
     for head in range(HEADS):
         first = head * HEAD_DIM
         lo = first // 128 * 128
         hi = -(-(first + HEAD_DIM) // 128) * 128
-        inside = lax.broadcasted_iota(jnp.int32, (length, hi - lo), 1) + lo
+        inside = lax.broadcasted_iota(jnp.int32, (hi - lo, length), 0) + lo
         inside = (inside >= first) & (inside < first + HEAD_DIM)
-        q_head = jnp.where(inside, q_s[:, lo:hi].astype(F32), 0.0).astype(BF16)
-        scores = lax.dot_general(
-            q_head, kv_s[:, lo:hi], (((1,), (1,)), ((), ())), preferred_element_type=F32
+        q_head = jnp.where(inside, qt_s[lo:hi, :].astype(F32), 0.0).astype(BF16)
+        scores = jnp.dot(k_s[:, lo:hi], q_head, preferred_element_type=F32)
+        hide = jnp.concatenate([hide_s[...]] * (length // 128), axis=1)
+        scores = scores * factor + hide
+        top = jnp.max(scores, axis=0, keepdims=True)
+        expo = jnp.exp2(scores - top)
+        total = jnp.sum(expo, axis=0, keepdims=True)
+        context = jnp.dot(
+            vt_s[first : first + HEAD_DIM, :], expo.astype(BF16), preferred_element_type=F32
         )
-        scores = scores * factor + hide
-        top = jnp.max(scores, axis=1, keepdims=True)
-        expo = jnp.exp2(scores - top)
-        total = jnp.sum(expo, axis=1, keepdims=True)
-        context = jnp.dot(
-            expo.astype(BF16), kv_s[:, width + lo : width + hi], preferred_element_type=F32
-        )
-        context = context / total
-        ctx_s[:, lo:hi] = jnp.where(inside, context, ctx_s[:, lo:hi].astype(F32)).astype(BF16)
-        if head == 1:
+        ctxt_s[first : first + HEAD_DIM, :] = (context / total).astype(BF16)
+        if head in (2, 6):
             advance()
-        if head == 6:
-            advance()
-    ready(1)
+
+    @tiles(width)
+    def _(at):
+        ctx_s[:, at(0)] = ctxt_s[at(0), :].astype(F32).T.astype(BF16)
+
+    ready(3)
 
     @pl.loop(0, mid_s.shape[1] // TILE)
     def _(j):
@@ -420,7 +422,7 @@
         mid_s[:, cols] = (frames_ref[:, cols].astype(F32) + add).astype(BF16)
 
     norm_rows(mid_s, gain_c_ref, normc_s)
-    ready(2)
+    ready(4, 5)
 
     half_width = w_glu.shape[1] // 2
     live = lax.broadcasted_iota(jnp.int32, (length, 1), 0) < count_ref[0]
@@ -467,7 +469,7 @@
     def _():
         gpad[16 + length : 32 + length, :] = jnp.zeros((16, half_width), F32)
 
-    finish(3)
+    finish(6)
     strip = 128
 
     @pl.loop(0, half_width // 128)
@@ -483,7 +485,7 @@
             pre = conv * scale_ref[:, cols] + shift_ref[:, cols]
             act_s[start : start + strip, cols] = (pre * jax.nn.sigmoid(pre)).astype(BF16)
 
-    ready(3)
+    ready(6)
 
     @pl.loop(0, out_ref.shape[1] // TILE)
     def _(j):
@@ -545,8 +547,11 @@
             pltpu.VMEM((half, model), BF16),
             pltpu.VMEM((3 * length, model), BF16),
             pltpu.VMEM((3, 8, 128), jnp.int32),
-            pltpu.VMEM((length, width), BF16),
-            pltpu.VMEM((3 * length, 2 * width), BF16),
+            pltpu.VMEM((3 * length, 128), F32),
+            pltpu.VMEM((width, length), BF16),
+            pltpu.VMEM((3 * length, width), BF16),
+            pltpu.VMEM((width, 3 * length), BF16),
+            pltpu.VMEM((width, length), BF16),
             pltpu.VMEM((length, width), BF16),
             pltpu.VMEM((length, model), BF16),
             pltpu.VMEM((length, model), BF16),
@@ -554,9 +559,9 @@
             pltpu.VMEM((length, half), BF16),
             pltpu.VMEM((2, 16, half), BF16),
             pltpu.VMEM((2, 16, half), BF16),
-            dma((6, chips - 1)), dma((6, chips - 1)),
-            dma((6, chips - 1)), dma((6, chips - 1)),
-            dma((6, chips)), dma((6, chips)),
+            dma((7, chips - 1)), dma((7, chips - 1)),
+            dma((7, chips - 1)), dma((7, chips - 1)),
+            dma((7, chips)), dma((7, chips)),
             dma((3,)), dma((2,)), dma((2,)), dma((2,)), dma((2,)), dma((2,)),
         ],
         compiler_params=pltpu.CompilerParams(

time: 114 us -> 119 us (1.044); the launches traced: 114 us -> 117 us
  Pallas kernels: 111 us -> 115 us
    pallas_call x1, Pallas kernels: 111 us -> 115 us  [fused(): pl.pallas_call(functools.partial(block, n), out_shape=jax.ShapeDtypeStruc...]
where the time goes in v3:
time: 119 us; the launch traced here: 117 us
  Pallas kernels  115 us (97%)
  local copies, waits for them, and re-layouts  2.06 us (2%)
    pallas_call x1, Pallas kernels, fused(): pl.pallas_call(functools.partial(block, n), out_shape=jax.ShapeDtypeStruc...  115 us

profile of v3, /device:TPU:1, one launch (start us, length us, event | category | flops | bytes accessed | tf_op | source)
XLA Modules:
  0.0 117.3 jit_solution(5659348607292982378)
XLA Ops:
  0.7 114.6 %shard_map.136 = bf16[256,1536]{1,0:T(8,128)(2,1)} custom-call(bf16[256,1536]{1,0:T(8,128)(2,1)} %frames_ref.1, s32[1]{0:T(128)S(6)} %copy.16.count_ref, s32[1,4]{1,0:T(1,128)} %look_ref.1, f32[1536]{0:T(1024)} %gain_a_ref.1, bf16[96,768]{1,0:T(8,128)(2,1)} %wq_ref.1, bf16[96,768]{1,0:T(8,128)(2,1)} %wk_ref.1, bf16[96,768]{1,0:T(8,128)(2,1)} %wv_ref.1, ...), custom_call_target="tpu_custom_call" | custom-call | flops 4831838208 | bytes 18874368 | tf_op jit(solution)/shard_map/pallas_call | solution.py:538
  115.3 2.1 %copy.17 = bf16[256,1536]{1,0:T(8,128)(2,1)} copy(bf16[256,1536]{1,0:T(8,128)(2,1)} %shard_map.136) | data formatting | bytes 1572864

commit v4 on v2

--- a/solution.py
+++ b/solution.py
@@ -183,23 +183,25 @@
 
     weights = (w_qkv, w_out, w_glu, w_proj)
     depth = tuple(w.shape[0] // n for w in weights)
-    full = tuple(w.shape[1] for w in weights)
-    around_cols = tuple((61 * c + 6400) // 12800 * 128 for c in full)
-    pieces = tuple(
-        (w, start, size)
-        for w, parts in enumerate((2, 1, 2, 1))
-        for size in [depth[w] // parts if depth[w] % (16 * parts) == 0 else depth[w]]
-        for start in range(0, depth[w], size)
+    width = wq_ref.shape[1]
+    part_q, part_g = width // 2, w_glu.shape[1] // 4
+    pieces = (
+        (0, 0, 3 * part_q, 55),
+        (0, 3 * part_q, 3 * part_q, 55),
+        (1, 0, w_out.shape[1], 61),
+        (2, 0, 2 * part_g, 61),
+        (2, 2 * part_g, 2 * part_g, 61),
+        (3, 0, w_proj.shape[1], 61),
     )
 
     def rows(p, owner, start, size):
-        w, low, high = pieces[p]
-        at = pl.ds(pl.multiple_of(owner * depth[w] + low, 16), high)
-        return weights[w].at[at, pl.ds(pl.multiple_of(start, 128), size)]
+        w, first = pieces[p][:2]
+        at = pl.ds(pl.multiple_of(owner * depth[w], 16), depth[w])
+        return weights[w].at[at, pl.ds(pl.multiple_of(first + start, 128), size)]
 
     def sizes(p):
-        w = pieces[p][0]
-        return full[w], around_cols[w]
+        cols, share = pieces[p][2:]
+        return cols, (share * cols + 6400) // 12800 * 128
 
     def copy(src, dst, send, recv, device):
         return pltpu.make_async_remote_copy(
@@ -255,7 +257,7 @@
                 over_x(w, side, hop).wait_recv()
                 over_core(w, hop + side * hops_a, arrived(side, hop)).start()
 
-    turns = (0, 0, 2, 3, 4, 5)
+    turns = (0, 1, 3, 4, 5, 6)
 
     def advance():
         number = len(rounds)
@@ -269,21 +271,15 @@
             if 0 < hop <= hops_a:
                 spread(p, hop - 1)
 
-    def finish(w):
-        for p, piece in enumerate(pieces):
-            if piece[0] == w:
-                while (p, hops_a - 1) not in stepped:
-                    advance()
-        for p, piece in enumerate(pieces):
-            if piece[0] == w:
-                spread(p, hops_a - 1)
-
-    def ready(w):
-        finish(w)
-        for p, piece in enumerate(pieces):
-            if piece[0] == w:
-                for slot in range(chips):
-                    over_core(p, slot, t).wait_recv()
+    def finish(p):
+        while (p, hops_a - 1) not in stepped:
+            advance()
+        spread(p, hops_a - 1)
+
+    def ready(p):
+        finish(p)
+        for slot in range(chips):
+            over_core(p, slot, t).wait_recv()
 
     barrier = pltpu.get_barrier_semaphore()
     around = [lax.rem(t + n + d, n) for d in (1, -1, 2, -2)]
@@ -291,12 +287,15 @@
         pl.semaphore_signal(barrier, inc=1, device_id=device, device_id_type=MESH)
 
     own = lambda w: pl.ds(pl.multiple_of(t * depth[w], 16), depth[w])
-    width = wq_ref.shape[1]
-    w_qkv[own(0), 0:width] = wq_ref[...]
-    w_qkv[own(0), width : 2 * width] = wk_ref[...]
-    w_qkv[own(0), 2 * width : 3 * width] = wv_ref[...]
+    for half in range(2):
+        for i, ref in enumerate((wk_ref, wv_ref, wq_ref)):
+            first = (3 * half + i) * part_q
+            w_qkv[own(0), first : first + part_q] = ref[:, half * part_q : (half + 1) * part_q]
+        for i in range(2):
+            first = (2 * half + i) * part_g
+            there = (2 * i + half) * part_g
+            w_glu[own(2), first : first + part_g] = wg_ref[:, there : there + part_g]
     w_out[own(1), :] = wo_ref[...]
-    w_glu[own(2), :] = wg_ref[...]
     w_proj[own(3), :] = wp_ref[...]
     pl.semaphore_wait(barrier, 8)
     advance()
@@ -355,28 +354,6 @@
         far.wait_recv()
         far_count.wait_recv()
 
-    ready(0)
-
-    @pl.loop(0, width // TILE)
-    def _(j):
-        cols = pl.ds(pl.multiple_of(j * TILE, TILE), TILE)
-        q_s[:, cols] = jnp.dot(
-            norm[2 * length : 3 * length, :], w_qkv[:, cols], preferred_element_type=F32
-        ).astype(BF16)
-
-    def spans(base):
-        @pl.loop(0, width // TILE)
-        def _(j):
-            cols = pl.ds(pl.multiple_of(base + j * TILE, TILE), TILE)
-            source = pl.ds(pl.multiple_of(base + width + j * TILE, TILE), TILE)
-            kv_s[:, cols] = jnp.dot(
-                norm[...], w_qkv[:, source], preferred_element_type=F32
-            ).astype(BF16)
-
-    spans(0)
-    advance()
-    spans(width)
-
     lane = lax.broadcasted_iota(jnp.int32, (1, 128), 1)
     hide = []
     for b in range(3 * length // 128):
@@ -388,30 +365,60 @@
     hide = jnp.concatenate(hide, axis=1)
     factor = math.log2(math.e) / math.sqrt(HEAD_DIM)
 
-    for head in range(HEADS):
-        first = head * HEAD_DIM
+    def project(half):
+        base = 3 * half * part_q
+
+        @pl.loop(0, 2 * part_q // TILE)
+        def _(j):
+            cols = pl.ds(pl.multiple_of(2 * half * part_q + j * TILE, TILE), TILE)
+            source = pl.ds(pl.multiple_of(base + j * TILE, 128), TILE)
+            kv_s[:, cols] = jnp.dot(
+                norm[...], w_qkv[:, source], preferred_element_type=F32
+            ).astype(BF16)
+
+        q_s[:, half * part_q : (half + 1) * part_q] = jnp.dot(
+            norm[2 * length :, :],
+            w_qkv[:, base + 2 * part_q : base + 3 * part_q],
+            preferred_element_type=F32,
+        ).astype(BF16)
+
+    def attend_head(head):
+        half, first = head // (HEADS // 2), head % (HEADS // 2) * HEAD_DIM
         lo = first // 128 * 128
         hi = -(-(first + HEAD_DIM) // 128) * 128
         inside = lax.broadcasted_iota(jnp.int32, (length, hi - lo), 1) + lo
         inside = (inside >= first) & (inside < first + HEAD_DIM)
-        q_head = jnp.where(inside, q_s[:, lo:hi].astype(F32), 0.0).astype(BF16)
+        q_at = slice(half * part_q + lo, half * part_q + hi)
+        k_at = slice(2 * half * part_q + lo, 2 * half * part_q + hi)
+        v_at = slice((2 * half + 1) * part_q + lo, (2 * half + 1) * part_q + hi)
+        q_head = jnp.where(inside, q_s[:, q_at].astype(F32), 0.0).astype(BF16)
         scores = lax.dot_general(
-            q_head, kv_s[:, lo:hi], (((1,), (1,)), ((), ())), preferred_element_type=F32
+            q_head, kv_s[:, k_at], (((1,), (1,)), ((), ())), preferred_element_type=F32
         )
         scores = scores * factor + hide
         top = jnp.max(scores, axis=1, keepdims=True)
         expo = jnp.exp2(scores - top)
         total = jnp.sum(expo, axis=1, keepdims=True)
-        context = jnp.dot(
-            expo.astype(BF16), kv_s[:, width + lo : width + hi], preferred_element_type=F32
-        )
+        context = jnp.dot(expo.astype(BF16), kv_s[:, v_at], preferred_element_type=F32)
         context = context / total
-        ctx_s[:, lo:hi] = jnp.where(inside, context, ctx_s[:, lo:hi].astype(F32)).astype(BF16)
+        ctx_s[:, q_at] = jnp.where(inside, context, ctx_s[:, q_at].astype(F32)).astype(BF16)
+
+    heads = HEADS // 2
+    ready(0)
+    project(0)
+    advance()
+    for head in range(heads):
+        attend_head(head)
         if head == 1:
             advance()
-        if head == 6:
+    ready(1)
+    project(1)
+    advance()
+    for head in range(heads, HEADS):
+        attend_head(head)
+        if head == heads + 1:
             advance()
-    ready(1)
+    ready(2)
 
     @pl.loop(0, mid_s.shape[1] // TILE)
     def _(j):
@@ -420,70 +427,87 @@
         mid_s[:, cols] = (frames_ref[:, cols].astype(F32) + add).astype(BF16)
 
     norm_rows(mid_s, gain_c_ref, normc_s)
-    ready(2)
-
-    half_width = w_glu.shape[1] // 2
+    ready(3)
+
+    half_width = 2 * part_g
     live = lax.broadcasted_iota(jnp.int32, (length, 1), 0) < count_ref[0]
 
-    @pl.loop(0, half_width // TILE)
-    def _(j):
-        cols = pl.ds(pl.multiple_of(j * TILE, TILE), TILE)
-        gate_cols = pl.ds(pl.multiple_of(j * TILE + half_width, TILE), TILE)
-        left = jnp.dot(normc_s[...], w_glu[:, cols], preferred_element_type=F32)
-        gate = jnp.dot(normc_s[...], w_glu[:, gate_cols], preferred_element_type=F32)
-        gated = jnp.where(live, left * jax.nn.sigmoid(gate), 0.0).astype(BF16)
-        gpad[16 : 16 + length, cols] = gated.astype(F32)
-        hsend[0, :, cols] = gated[0:16]
-        hsend[1, :, cols] = gated[length - 16 : length]
-
-    below = copy(hsend.at[1], hrecv.at[0], h_send.at[0], h_recv.at[0], here(t + 1))
-    above = copy(hsend.at[0], hrecv.at[1], h_send.at[1], h_recv.at[1], here(t - 1))
-
-    @pl.when(t + 1 < n)
-    def _():
-        below.start()
-
-    @pl.when(t >= 1)
-    def _():
-        above.start()
-
-    advance()
-
-    @pl.when(t >= 1)
-    def _():
-        below.wait_recv()
-        gpad[0:16, :] = hrecv[0].astype(F32)
-
-    @pl.when(t < 1)
-    def _():
-        gpad[0:16, :] = jnp.zeros((16, half_width), F32)
-
-    @pl.when(t + 1 < n)
-    def _():
-        above.wait_recv()
-        gpad[16 + length : 32 + length, :] = hrecv[1].astype(F32)
-
-    @pl.when(t + 1 >= n)
-    def _():
-        gpad[16 + length : 32 + length, :] = jnp.zeros((16, half_width), F32)
-
-    finish(3)
+    def gate(half):
+        @pl.loop(0, part_g // TILE)
+        def _(j):
+            cols = pl.ds(pl.multiple_of(half * part_g + j * TILE, TILE), TILE)
+            left_cols = pl.ds(pl.multiple_of(2 * half * part_g + j * TILE, TILE), TILE)
+            gate_cols = pl.ds(pl.multiple_of((2 * half + 1) * part_g + j * TILE, TILE), TILE)
+            left = jnp.dot(normc_s[...], w_glu[:, left_cols], preferred_element_type=F32)
+            right = jnp.dot(normc_s[...], w_glu[:, gate_cols], preferred_element_type=F32)
+            gated = jnp.where(live, left * jax.nn.sigmoid(right), 0.0).astype(BF16)
+            gpad[16 : 16 + length, cols] = gated.astype(F32)
+            hsend[0, :, cols] = gated[0:16]
+            hsend[1, :, cols] = gated[length - 16 : length]
+
+    def halo(half, side):
+        cols = pl.ds(half * part_g, part_g)
+        return copy(
+            hsend.at[1 - side, :, cols], hrecv.at[side, :, cols],
+            h_send.at[half, side], h_recv.at[half, side], here(t + 1 - 2 * side),
+        )
+
+    def send_halo(half):
+
+        @pl.when(t + 1 < n)
+        def _():
+            halo(half, 0).start()
+
+        @pl.when(t >= 1)
+        def _():
+            halo(half, 1).start()
+
     strip = 128
 
-    @pl.loop(0, half_width // 128)
-    def _(j):
-        cols = pl.ds(pl.multiple_of(j * 128, 128), 128)
-        for start in range(0, length, strip):
-            conv = jnp.zeros((strip, 128), F32)
-            for shift in range(8):
-                moved = gpad[start + shift : start + shift + strip + 24, cols]
-                for at in range(shift, 32, 8):
-                    if at >= 1:
-                        conv = conv + taps_ref[at - 1 : at, cols] * moved[at - shift : at - shift + strip]
-            pre = conv * scale_ref[:, cols] + shift_ref[:, cols]
-            act_s[start : start + strip, cols] = (pre * jax.nn.sigmoid(pre)).astype(BF16)
-
-    ready(3)
+    def convolve(half):
+        cols = pl.ds(half * part_g, part_g)
+
+        @pl.when(t >= 1)
+        def _():
+            halo(half, 0).wait_recv()
+            gpad[0:16, cols] = hrecv[0, :, cols].astype(F32)
+
+        @pl.when(t < 1)
+        def _():
+            gpad[0:16, cols] = jnp.zeros((16, part_g), F32)
+
+        @pl.when(t + 1 < n)
+        def _():
+            halo(half, 1).wait_recv()
+            gpad[16 + length : 32 + length, cols] = hrecv[1, :, cols].astype(F32)
+
+        @pl.when(t + 1 >= n)
+        def _():
+            gpad[16 + length : 32 + length, cols] = jnp.zeros((16, part_g), F32)
+
+        @pl.loop(0, part_g // 128)
+        def _(j):
+            cols = pl.ds(pl.multiple_of(half * part_g + j * 128, 128), 128)
+            for start in range(0, length, strip):
+                conv = jnp.zeros((strip, 128), F32)
+                for shift in range(8):
+                    moved = gpad[start + shift : start + shift + strip + 24, cols]
+                    for at in range(shift, 32, 8):
+                        if at >= 1:
+                            conv = conv + taps_ref[at - 1 : at, cols] * moved[at - shift : at - shift + strip]
+                pre = conv * scale_ref[:, cols] + shift_ref[:, cols]
+                act_s[start : start + strip, cols] = (pre * jax.nn.sigmoid(pre)).astype(BF16)
+
+    gate(0)
+    send_halo(0)
+    finish(4)
+    convolve(0)
+    ready(4)
+    gate(1)
+    send_halo(1)
+    finish(5)
+    convolve(1)
+    ready(5)
 
     @pl.loop(0, out_ref.shape[1] // TILE)
     def _(j):
@@ -503,11 +527,13 @@
     def _():
         near.wait_send()
         near_count.wait_send()
-        below.wait_send()
+        for half in range(2):
+            halo(half, 0).wait_send()
 
     @pl.when(t >= 1)
     def _():
-        above.wait_send()
+        for half in range(2):
+            halo(half, 1).wait_send()
 
     @pl.when(t + 2 < n)
     def _():
@@ -557,7 +583,7 @@
             dma((6, chips - 1)), dma((6, chips - 1)),
             dma((6, chips - 1)), dma((6, chips - 1)),
             dma((6, chips)), dma((6, chips)),
-            dma((3,)), dma((2,)), dma((2,)), dma((2,)), dma((2,)), dma((2,)),
+            dma((3,)), dma((2,)), dma((2,)), dma((2,)), dma((2, 2)), dma((2, 2)),
         ],
         compiler_params=pltpu.CompilerParams(
             collective_id=0, has_side_effects=True, vmem_limit_bytes=56 * 1024 * 1024
@@ -578,7 +604,7 @@
     whole = all(w.shape[0] % 16 == 0 and w.shape[0] >= 48 for w in (w_query, w_out, w_glu, w_proj))
     tiles = all(
         w.shape[1] % TILE == 0 for w in (w_query, w_out, w_proj)
-    ) and w_glu.shape[1] % (2 * TILE) == 0
+    ) and w_glu.shape[1] % (4 * TILE) == 0
     if groups == 2 and n % 8 == 0 and whole and tiles and frames.shape[0] % 256 == 0:
         return fused(n, *args)
     return plain(*args)

time: 114 us -> 115 us (level)
  no operation moved by 1% of the time
where the time goes in v4:
time: 115 us; the launch traced here: 114 us
  Pallas kernels  112 us (97%)
  local copies, waits for them, and re-layouts  2.06 us (2%)
    pallas_call x1, Pallas kernels, fused(): pl.pallas_call(functools.partial(block, n), out_shape=jax.ShapeDtypeStruc...  112 us

profile of v4, /device:TPU:1, one launch (start us, length us, event | category | flops | bytes accessed | tf_op | source)
XLA Modules:
  0.0 114.3 jit_solution(2218907112593412065)
XLA Ops:
  0.7 111.6 %shard_map.136 = bf16[256,1536]{1,0:T(8,128)(2,1)} custom-call(bf16[256,1536]{1,0:T(8,128)(2,1)} %frames_ref.1, s32[1]{0:T(128)S(6)} %copy.16.count_ref, s32[1,4]{1,0:T(1,128)} %look_ref.1, f32[1536]{0:T(1024)} %gain_a_ref.1, bf16[96,768]{1,0:T(8,128)(2,1)} %wq_ref.1, bf16[96,768]{1,0:T(8,128)(2,1)} %wk_ref.1, bf16[96,768]{1,0:T(8,128)(2,1)} %wv_ref.1, ...), custom_call_target="tpu_custom_call" | custom-call | flops 4831838208 | bytes 18874368 | tf_op jit(solution)/shard_map/pallas_call | solution.py:562
  112.3 2.1 %copy.17 = bf16[256,1536]{1,0:T(8,128)(2,1)} copy(bf16[256,1536]{1,0:T(8,128)(2,1)} %shard_map.136) | data formatting | bytes 1572864

commit v5 on v0

--- a/solution.py
+++ b/solution.py
@@ -1,8 +1,11 @@
+import functools
 import math
 
 import jax
 import jax.numpy as jnp
 from jax import lax
+from jax.experimental import pallas as pl
+from jax.experimental.pallas import tpu as pltpu
 from jax.sharding import PartitionSpec as P
 
 HEADS = 8
@@ -75,7 +78,7 @@
     return jnp.transpose(stacked, (1, 0, 2)).reshape(width, HEADS * HEAD_DIM)
 
 
-def shards(
+def plain(
     frames,
     frame_count,
     lookback_mask,
@@ -129,9 +132,502 @@
     return (mid.astype(jnp.float32) + conv_sum).astype(jnp.bfloat16)
 
 
+F32 = jnp.float32
+BF16 = jnp.bfloat16
+MESH = pl.DeviceIdType.MESH
+TILE = 256
+
+
+def norm_rows(source, gain_ref, target):
+    rows = source.shape[0]
+
+    @pl.loop(0, rows // 32)
+    def _(step):
+        at = pl.ds(pl.multiple_of(step * 32, 32), 32)
+        xf = source[at, :].astype(F32)
+        mean = jnp.mean(xf, axis=-1, keepdims=True)
+        centered = xf - mean
+        var = jnp.mean(centered * centered, axis=-1, keepdims=True)
+        target[at, :] = (centered * lax.rsqrt(var + 1e-05) * gain_ref[...].reshape(1, -1)).astype(BF16)
+
+
+def block(
+    n,
+    frames_ref, count_ref, look_ref, gain_a_ref, wq_ref, wk_ref, wv_ref, wo_ref, gain_c_ref,
+    wg_ref, taps_ref, scale_ref, shift_ref, wp_ref,
+    out_ref,
+    w_qkv, w_out, w_glu, w_proj, g_qkv, g_out, g_glu, g_proj, g_frames, res, norm, meta,
+    q_s, kv_s, ctx_s, mid_s, normc_s, gpad, act_s, hsend, hrecv, osend, orecv,
+    ring_send, ring_recv, x_send, x_recv, c_send, c_recv, n_send, n_recv, m_send, m_recv,
+    h_send, h_recv, e_send, e_recv,
+):
+    g = lax.axis_index("groups")
+    t = lax.axis_index("tm")
+    core = lax.rem(t, 2)
+    other = 1 - core
+    chip = t // 2
+    chips = n // 2
+    deep = chips // 2
+    hops_a, hops_b = chips // 2, chips // 2 - 1
+    place = jnp.where(lax.rem(chip, 2) == 0, chip // 2, chips - 1 - chip // 2)
+    turn = 1 - 2 * core
+
+    def at_place(r):
+        r = lax.rem(r + 2 * chips, chips)
+        return jnp.where(r < deep, 2 * r, 2 * (chips - 1 - r) + 1)
+
+    here = lambda index: (g, index)
+    next_a = here(2 * at_place(place + turn) + core)
+    next_b = here(2 * at_place(place - turn) + core)
+    pair = here(t + turn)
+    across = (1 - g, t)
+
+    weights = (w_qkv, w_out, w_glu, w_proj)
+    depth = tuple(w.shape[0] // n for w in weights)
+    length, model = frames_ref.shape
+    part_q, part_d, part_g = wq_ref.shape[1] // 2, model // 2, wg_ref.shape[1] // 4
+    pieces = (
+        (0, 0, 2 * part_q, 50),
+        (0, 2 * part_q, part_q, 66),
+        (1, 0, part_d, 66),
+        (2, 0, part_g, 50),
+        (2, part_g, part_g, 75),
+        (3, 0, part_d, 66),
+    )
+    turns = (0, 0, 2, 3, 3, 4)
+
+    def rows(p, owner, start, size):
+        w, first = pieces[p][:2]
+        at = pl.ds(pl.multiple_of(owner * 2 * depth[w], 16), 2 * depth[w])
+        return weights[w].at[at, pl.ds(pl.multiple_of(first + start, 128), size)]
+
+    def sizes(p):
+        cols, share = pieces[p][2:]
+        return cols, (share * cols + 6400) // 12800 * 128
+
+    def copy(src, dst, send, recv, device):
+        return pltpu.make_async_remote_copy(
+            src_ref=src, dst_ref=dst, send_sem=send, recv_sem=recv,
+            device_id=device, device_id_type=MESH,
+        )
+
+    def ring(p, side, hop):
+        sign = turn if side == 0 else -turn
+        cols, ringed = sizes(p)
+        view = rows(p, at_place(place - sign * hop), g * (cols - ringed), ringed)
+        slot = hop + side * hops_a
+        target = next_a if side == 0 else next_b
+        return copy(view, view, ring_send.at[p, slot], ring_recv.at[p, slot], target)
+
+    def over_x(p, side, hop):
+        owner = at_place(place - (turn if side == 0 else -turn) * (hop + 1))
+        cols, ringed = sizes(p)
+        view = rows(p, owner, g * ringed, cols - ringed)
+        slot = hop + side * hops_a
+        return copy(view, view, x_send.at[p, slot], x_recv.at[p, slot], across)
+
+    sides = ((0, hops_a), (1, hops_b))
+    own = lambda w: pl.ds(pl.multiple_of(t * depth[w], 16), depth[w])
+    given = (g_qkv, g_out, g_glu, g_proj)
+
+    def give(w):
+        return copy(given[w], weights[w].at[own(w), :], c_send.at[w], c_recv.at[w], pair)
+
+    got, stepped, rounds = set(), set(), []
+
+    def begin(p):
+        w = pieces[p][0]
+        if w not in got:
+            got.add(w)
+            give(w).wait_recv()
+        ring(p, 0, 0).start()
+        ring(p, 1, 0).start()
+
+    def step(p, hop):
+        stepped.add((p, hop))
+        for side, hops in sides:
+            if hop < hops:
+                ring(p, side, hop).wait_recv()
+                if hop + 1 < hops:
+                    ring(p, side, hop + 1).start()
+                over_x(p, side, hop).start()
+
+    def advance():
+        number = len(rounds)
+        rounds.append(number)
+        for p, first in enumerate(turns):
+            hop = number - first - 1
+            if hop == -1:
+                begin(p)
+            if 0 <= hop < hops_a:
+                step(p, hop)
+
+    def ready(*which):
+        for p in which:
+            while (p, hops_a - 1) not in stepped:
+                advance()
+        for p in which:
+            for side, hops in sides:
+                for hop in range(hops):
+                    over_x(p, side, hop).wait_recv()
+
+    barrier = pltpu.get_barrier_semaphore()
+    around = [here(lax.rem(t + n + d, n)) for d in (2, -2)]
+    for device in [next_a, next_b, pair, across] + around:
+        pl.semaphore_signal(barrier, inc=1, device_id=device, device_id_type=MESH)
+
+    def half_of(ref, which, first, size):
+        return ref[:, pl.ds(pl.multiple_of(first + which * size, 128), size)]
+
+    for i, ref in enumerate((wk_ref, wv_ref, wq_ref)):
+        cols = slice(i * part_q, (i + 1) * part_q)
+        w_qkv[own(0), cols] = half_of(ref, core, 0, part_q)
+        g_qkv[:, cols] = half_of(ref, other, 0, part_q)
+    w_out[own(1), :] = half_of(wo_ref, core, 0, part_d)
+    g_out[...] = half_of(wo_ref, other, 0, part_d)
+    for i in range(2):
+        cols = slice(i * part_g, (i + 1) * part_g)
+        w_glu[own(2), cols] = half_of(wg_ref, core, 2 * i * part_g, part_g)
+        g_glu[:, cols] = half_of(wg_ref, other, 2 * i * part_g, part_g)
+    w_proj[own(3), :] = half_of(wp_ref, core, 0, part_d)
+    g_proj[...] = half_of(wp_ref, other, 0, part_d)
+    res[core] = half_of(frames_ref, core, 0, part_d)
+    g_frames[...] = half_of(frames_ref, other, 0, part_d)
+    pl.semaphore_wait(barrier, 6)
+    for w in range(4):
+        give(w).start()
+    swap_res = copy(g_frames, res.at[core], e_send.at[0], e_recv.at[0], pair)
+    advance()
+
+    mine = 2 + core
+    norm_rows(frames_ref, gain_a_ref, norm.at[mine])
+    meta[mine, 0:1, :] = jnp.full((1, 128), count_ref[0], jnp.int32)
+    for b in range(4):
+        meta[mine, 1 + b : 2 + b, :] = jnp.full((1, 128), look_ref[0, b], jnp.int32)
+    norm_pair = copy(norm.at[mine], norm.at[mine], n_send.at[0], n_recv.at[0], pair)
+    norm_next = copy(norm.at[mine], norm.at[core], n_send.at[1], n_recv.at[1], here(t + 2))
+    norm_relay = copy(norm.at[core], norm.at[core], n_send.at[2], n_recv.at[2], pair)
+    meta_pair = copy(meta.at[mine], meta.at[mine], m_send.at[0], m_recv.at[0], pair)
+    meta_next = copy(meta.at[mine], meta.at[core], m_send.at[1], m_recv.at[1], here(t + 2))
+    meta_relay = copy(meta.at[core], meta.at[core], m_send.at[2], m_recv.at[2], pair)
+
+    @pl.when(t + 2 < n)
+    def _():
+        norm_next.start()
+        meta_next.start()
+
+    norm_pair.start()
+    meta_pair.start()
+    swap_res.start()
+
+    @pl.when(t < 2)
+    def _():
+        for i in range(2):
+            norm[i] = jnp.zeros(norm.shape[1:], BF16)
+            meta[i] = jnp.zeros(meta.shape[1:], jnp.int32)
+
+    advance()
+    advance()
+
+    @pl.when(t >= 2)
+    def _():
+        norm_next.wait_recv()
+        meta_next.wait_recv()
+        norm_relay.start()
+        meta_relay.start()
+
+    norm_pair.wait_recv()
+    meta_pair.wait_recv()
+    swap_res.wait_recv()
+    advance()
+
+    @pl.when(t >= 2)
+    def _():
+        norm_relay.wait_recv()
+        meta_relay.wait_recv()
+
+    ready(0)
+
+    @pl.loop(0, 2 * part_q // TILE)
+    def _(j):
+        cols = pl.ds(pl.multiple_of(j * TILE, TILE), TILE)
+        for i in range(4):
+            kv_s[i * length : (i + 1) * length, cols] = jnp.dot(
+                norm[i], w_qkv[:, cols], preferred_element_type=F32
+            ).astype(BF16)
+
+    ready(1)
+    for i in range(2):
+        q_s[i * length : (i + 1) * length, :] = jnp.dot(
+            norm[2 + i], w_qkv[:, 2 * part_q :], preferred_element_type=F32
+        ).astype(BF16)
+    advance()
+
+    lane = lax.broadcasted_iota(jnp.int32, (1, 128), 1)
+
+    def hidden(span):
+        hide = []
+        for b in range(3 * length // 128):
+            limit = meta[span + b * 128 // length][0:1, :] - b * 128 % length
+            seen = lane < limit
+            if b * 128 < 2 * length:
+                allowed = 1 + b * 128 // (length // 2)
+                seen = seen & (meta[2 + span][allowed : allowed + 1, :] > 0)
+            hide.append(jnp.where(seen, 0.0, -1e30))
+        return jnp.concatenate(hide, axis=1)
+
+    factor = math.log2(math.e) / math.sqrt(HEAD_DIM)
+
+    def attend_head(span, head, hide):
+        first = head * HEAD_DIM
+        lo = first // 128 * 128
+        hi = -(-(first + HEAD_DIM) // 128) * 128
+        inside = lax.broadcasted_iota(jnp.int32, (length, hi - lo), 1) + lo
+        inside = (inside >= first) & (inside < first + HEAD_DIM)
+        q_at = slice(span * length, (span + 1) * length)
+        k_at = slice(span * length, (span + 3) * length)
+        q_head = jnp.where(inside, q_s[q_at, lo:hi].astype(F32), 0.0).astype(BF16)
+        scores = lax.dot_general(
+            q_head, kv_s[k_at, lo:hi], (((1,), (1,)), ((), ())), preferred_element_type=F32
+        )
+        scores = scores * factor + hide
+        top = jnp.max(scores, axis=1, keepdims=True)
+        expo = jnp.exp2(scores - top)
+        total = jnp.sum(expo, axis=1, keepdims=True)
+        context = jnp.dot(
+            expo.astype(BF16), kv_s[k_at, part_q + lo : part_q + hi], preferred_element_type=F32
+        )
+        context = context / total
+        before = ctx_s[core, q_at, lo:hi].astype(F32)
+        ctx_s[core, q_at, lo:hi] = jnp.where(inside, context, before).astype(BF16)
+
+    ctx_s[core] = jnp.zeros(ctx_s.shape[1:], BF16)
+    for span in range(2):
+        hide = hidden(span)
+        for head in range(HEADS // 2):
+            attend_head(span, head, hide)
+            if head == 1:
+                advance()
+
+    swap_ctx = copy(ctx_s.at[core], ctx_s.at[core], e_send.at[1], e_recv.at[1], pair)
+    swap_ctx.start()
+    ready(2)
+    swap_ctx.wait_recv()
+
+    @pl.loop(0, part_d // TILE)
+    def _(j):
+        cols = pl.ds(pl.multiple_of(j * TILE, TILE), TILE)
+        add = jnp.dot(ctx_s[0], w_out[:part_q, cols], preferred_element_type=F32)
+        add = add + jnp.dot(ctx_s[1], w_out[part_q:, cols], preferred_element_type=F32)
+        for i in range(2):
+            at = slice(i * length, (i + 1) * length)
+            mid_s[core, at, cols] = (res[i, :, cols].astype(F32) + add[at]).astype(BF16)
+
+    swap_mid = copy(mid_s.at[core], mid_s.at[core], e_send.at[2], e_recv.at[2], pair)
+    swap_mid.start()
+    advance()
+    swap_mid.wait_recv()
+
+    @pl.loop(0, 2 * length // 32)
+    def _(j):
+        at = pl.ds(pl.multiple_of(j * 32, 32), 32)
+        xf = jnp.concatenate([mid_s[0, at, :], mid_s[1, at, :]], axis=1).astype(F32)
+        mean = jnp.mean(xf, axis=-1, keepdims=True)
+        centered = xf - mean
+        var = jnp.mean(centered * centered, axis=-1, keepdims=True)
+        gain = gain_c_ref[...].reshape(1, -1)
+        normc_s[at, :] = (centered * lax.rsqrt(var + 1e-05) * gain).astype(BF16)
+
+    ready(3, 4)
+
+    @pl.loop(0, part_g // TILE)
+    def _(j):
+        cols = pl.ds(pl.multiple_of(j * TILE, TILE), TILE)
+        gate_cols = pl.ds(pl.multiple_of(part_g + j * TILE, TILE), TILE)
+        for i in range(2):
+            at = slice(i * length, (i + 1) * length)
+            left = jnp.dot(normc_s[at, :], w_glu[:, cols], preferred_element_type=F32)
+            right = jnp.dot(normc_s[at, :], w_glu[:, gate_cols], preferred_element_type=F32)
+            live = lax.broadcasted_iota(jnp.int32, (length, 1), 0) < meta[2 + i][0:1, 0:1]
+            gated = jnp.where(live, left * jax.nn.sigmoid(right), 0.0).astype(BF16)
+            gpad[16 + i * length : 16 + (i + 1) * length, cols] = gated.astype(F32)
+            if i == 0:
+                hsend[0, :, cols] = gated[0:16]
+            else:
+                hsend[1, :, cols] = gated[length - 16 : length]
+
+    below = copy(hsend.at[1], hrecv.at[0], h_send.at[0], h_recv.at[0], here(t + 2))
+    above = copy(hsend.at[0], hrecv.at[1], h_send.at[1], h_recv.at[1], here(t - 2))
+
+    @pl.when(t + 2 < n)
+    def _():
+        below.start()
+
+    @pl.when(t >= 2)
+    def _():
+        above.start()
+
+    while (5, hops_a - 1) not in stepped:
+        advance()
+
+    @pl.when(t >= 2)
+    def _():
+        below.wait_recv()
+        gpad[0:16, :] = hrecv[0].astype(F32)
+
+    @pl.when(t < 2)
+    def _():
+        gpad[0:16, :] = jnp.zeros((16, part_g), F32)
+
+    @pl.when(t + 2 < n)
+    def _():
+        above.wait_recv()
+        gpad[16 + 2 * length : 32 + 2 * length, :] = hrecv[1].astype(F32)
+
+    @pl.when(t + 2 >= n)
+    def _():
+        gpad[16 + 2 * length : 32 + 2 * length, :] = jnp.zeros((16, part_g), F32)
+
+    strip = 128
+
+    @pl.loop(0, part_g // 128)
+    def _(j):
+        cols = pl.ds(pl.multiple_of(j * 128, 128), 128)
+        wide = pl.ds(pl.multiple_of(core * part_g + j * 128, 128), 128)
+        for start in range(0, 2 * length, strip):
+            conv = jnp.zeros((strip, 128), F32)
+            for shift in range(8):
+                moved = gpad[start + shift : start + shift + strip + 24, cols]
+                for at in range(shift, 32, 8):
+                    if at >= 1:
+                        conv = conv + taps_ref[at - 1 : at, wide] * moved[at - shift : at - shift + strip]
+            pre = conv * scale_ref[:, wide] + shift_ref[:, wide]
+            act_s[core, start : start + strip, cols] = (pre * jax.nn.sigmoid(pre)).astype(BF16)
+
+    swap_act = copy(act_s.at[core], act_s.at[core], e_send.at[3], e_recv.at[3], pair)
+    swap_act.start()
+    ready(5)
+    swap_act.wait_recv()
+
+    def result(span, cols):
+        at = pl.ds(pl.multiple_of(span * length, length), length)
+        add = jnp.dot(act_s[0, at, :], w_proj[:part_g, cols], preferred_element_type=F32)
+        add = add + jnp.dot(act_s[1, at, :], w_proj[part_g:, cols], preferred_element_type=F32)
+        return (mid_s[core, at, cols].astype(F32) + add).astype(BF16)
+
+    @pl.loop(0, part_d // TILE)
+    def _(j):
+        cols = pl.ds(pl.multiple_of(j * TILE, TILE), TILE)
+        osend[:, cols] = result(other, cols)
+
+    swap_out = copy(osend, orecv, e_send.at[4], e_recv.at[4], pair)
+    swap_out.start()
+
+    @pl.loop(0, part_d // TILE)
+    def _(j):
+        cols = pl.ds(pl.multiple_of(j * TILE, TILE), TILE)
+        wide = pl.ds(pl.multiple_of(core * part_d + j * TILE, TILE), TILE)
+        out_ref[:, wide] = result(core, cols)
+
+    swap_out.wait_recv()
+    out_ref[:, pl.ds(pl.multiple_of(other * part_d, 128), part_d)] = orecv[...]
+
+    for p in range(len(pieces)):
+        for side, hops in sides:
+            for hop in range(hops):
+                ring(p, side, hop).wait_send()
+                over_x(p, side, hop).wait_send()
+    for w in range(4):
+        give(w).wait_send()
+    for swap in (swap_res, swap_ctx, swap_mid, swap_act, swap_out, norm_pair, meta_pair):
+        swap.wait_send()
+
+    @pl.when(t + 2 < n)
+    def _():
+        norm_next.wait_send()
+        meta_next.wait_send()
+        below.wait_send()
+
+    @pl.when(t >= 2)
+    def _():
+        norm_relay.wait_send()
+        meta_relay.wait_send()
+        above.wait_send()
+
+
+def fused(
+    n, frames, frame_count, lookback_mask, attn_gain, w_query, w_key, w_value, w_out, conv_gain,
+    w_glu, depthwise, conv_scale, conv_shift, w_proj,
+):
+    length, model = frames.shape
+    width = w_query.shape[1]
+    half = w_glu.shape[1] // 2
+    chips = n // 2
+    inside, scalars = (pl.BlockSpec(memory_space=m) for m in (pltpu.VMEM, pltpu.SMEM))
+    dma = pltpu.SemaphoreType.DMA
+    params = 3 * width * model + model * width + 2 * half * model + half * model
+    return pl.pallas_call(
+        functools.partial(block, n),
+        out_shape=jax.ShapeDtypeStruct((length, model), BF16),
+        in_specs=[inside, scalars, scalars] + [inside] * 11,
+        out_specs=pl.BlockSpec(memory_space=pltpu.VMEM),
+        scratch_shapes=[
+            pltpu.VMEM((model, 3 * width // 2), BF16),
+            pltpu.VMEM((width, model // 2), BF16),
+            pltpu.VMEM((model, half), BF16),
+            pltpu.VMEM((half, model // 2), BF16),
+            pltpu.VMEM((model // n, 3 * width // 2), BF16),
+            pltpu.VMEM((width // n, model // 2), BF16),
+            pltpu.VMEM((model // n, half), BF16),
+            pltpu.VMEM((half // n, model // 2), BF16),
+            pltpu.VMEM((length, model // 2), BF16),
+            pltpu.VMEM((2, length, model // 2), BF16),
+            pltpu.VMEM((4, length, model), BF16),
+            pltpu.VMEM((4, 8, 128), jnp.int32),
+            pltpu.VMEM((2 * length, width // 2), BF16),
+            pltpu.VMEM((4 * length, width), BF16),
+            pltpu.VMEM((2, 2 * length, width // 2), BF16),
+            pltpu.VMEM((2, 2 * length, model // 2), BF16),
+            pltpu.VMEM((2 * length, model), BF16),
+            pltpu.VMEM((2 * length + 32, half // 2), F32),
+            pltpu.VMEM((2, 2 * length, half // 2), BF16),
+            pltpu.VMEM((2, 16, half // 2), BF16),
+            pltpu.VMEM((2, 16, half // 2), BF16),
+            pltpu.VMEM((length, model // 2), BF16),
+            pltpu.VMEM((length, model // 2), BF16),
+            dma((6, chips - 1)), dma((6, chips - 1)),
+            dma((6, chips - 1)), dma((6, chips - 1)),
+            dma((4,)), dma((4,)), dma((3,)), dma((3,)), dma((3,)), dma((3,)),
+            dma((2,)), dma((2,)), dma((5,)), dma((5,)),
+        ],
+        compiler_params=pltpu.CompilerParams(
+            collective_id=0, has_side_effects=True, vmem_limit_bytes=56 * 1024 * 1024
+        ),
+        cost_estimate=pl.CostEstimate(
+            flops=2 * length * params, bytes_accessed=2 * params, transcendentals=length * half
+        ),
+    )(
+        frames, frame_count, lookback_mask, attn_gain, w_query, w_key, w_value, w_out,
+        conv_gain, w_glu, depthwise, conv_scale.reshape(1, -1),
+        conv_shift.reshape(1, -1), w_proj,
+    )
+
+
+def shards(groups, *args):
+    n = lax.axis_size("tm")
+    frames, w_query, w_out, w_glu, w_proj = args[0], args[4], args[7], args[9], args[13]
+    whole = all(w.shape[0] % 16 == 0 and w.shape[0] >= 48 for w in (w_query, w_out, w_glu, w_proj))
+    tiles = all(
+        w.shape[1] % TILE == 0 for w in (w_query, w_out, w_proj)
+    ) and w_glu.shape[1] % (4 * TILE) == 0
+    if groups == 2 and n % 8 == 0 and whole and tiles and frames.shape[0] % 256 == 0:
+        return fused(n, *args)
+    return plain(*args)
+
+
 def solution(mesh):
     return jax.shard_map(
-        shards,
+        functools.partial(shards, mesh.shape["groups"]),
         mesh=mesh,
         in_specs=(
             P(("groups", "tm"), None),

time: 310 us -> 114 us (0.37)
  waiting for transfers between devices: 207 us -> 0 us
  Pallas kernels: 0 us -> 111 us
  matrix products: 43.7 us -> 0 us
  starting transfers between devices: 22.5 us -> 0 us
  between operations: 14.7 us -> 0.66 us
  other arithmetic: 7.51 us -> 0 us
  loops' own time: 5.63 us -> 0 us
  local copies, waits for them, and re-layouts: 7.22 us -> 2.06 us
    all_gather x6 -> x0, waiting for transfers between devices: 204 us -> none  [the longest x1 59.8 us: shards(): glu_in = add_rows(norm_c, lax.all_gather(w_glu, 'tm', axis=0, tiled=True))]
    pallas_call x0 -> x1, Pallas kernels: none -> 111 us  [fused(): pl.pallas_call(functools.partial(block, n), out_shape=jax.ShapeDtypeStruc...]
    dot_general x22 -> x0, matrix products: 43.7 us -> none  [the longest x6 23.8 us: add_rows(): return jnp.dot(left, piece, preferred_element_type=jnp.float32)]
    ppermute x8 -> x0, starting transfers between devices: 22.3 us -> none  [the longest x6 17.8 us: shifted(): return lax.ppermute(block, axis, route)]
    another operation x1 -> x0, loops' own time: 5.63 us -> none  [attend(): stacked = lax.map(one_head, jnp.arange(HEADS, dtype=jnp.int32))]
    dynamic_slice x8 -> x0, local copies, waits for them, and re-layouts: 5.3 us -> none  [attend(): stacked = lax.map(one_head, jnp.arange(HEADS, dtype=jnp.int32))]
    unnamed x6 -> x0, waiting for transfers between devices: 3.16 us -> none
    reduce_sum x12 -> x0, other arithmetic: 3.14 us -> none  [the longest x8 2.23 us: one_head(): weights = (expo / jnp.sum(expo, axis=1, keepdims=True)).astype(jnp.bfloat16)]
  transfers between devices with their start and end apart: 14 -> 0, of which waited for: 6 -> 0; matrix products, arithmetic and copies ran while one was open for 16% -> 0% of each run, Pallas kernels for 0% -> 0%
where the time goes in v5:
time: 114 us
  Pallas kernels  111 us (97%)
  local copies, waits for them, and re-layouts  2.06 us (2%)
    pallas_call x1, Pallas kernels, fused(): pl.pallas_call(functools.partial(block, n), out_shape=jax.ShapeDtypeStruc...  111 us

profile of v5, /device:TPU:1, one launch (start us, length us, event | category | flops | bytes accessed | tf_op | source)
XLA Modules:
  0.0 113.6 jit_solution(13374751852653384748)
XLA Ops:
  0.7 110.9 %shard_map.136 = bf16[256,1536]{1,0:T(8,128)(2,1)} custom-call(bf16[256,1536]{1,0:T(8,128)(2,1)} %frames_ref.1, s32[1]{0:T(128)S(6)} %copy.16.count_ref, s32[1,4]{1,0:T(1,128)} %look_ref.1, f32[1536]{0:T(1024)} %gain_a_ref.1, bf16[96,768]{1,0:T(8,128)(2,1)} %wq_ref.1, bf16[96,768]{1,0:T(8,128)(2,1)} %wk_ref.1, bf16[96,768]{1,0:T(8,128)(2,1)} %wv_ref.1, ...), custom_call_target="tpu_custom_call" | custom-call | flops 4831838208 | bytes 18874368 | tf_op jit(solution)/shard_map/pallas_call | solution.py:569
  111.5 2.1 %copy.17 = bf16[256,1536]{1,0:T(8,128)(2,1)} copy(bf16[256,1536]{1,0:T(8,128)(2,1)} %shard_map.136) | data formatting | bytes 1572864

commit v6 on v5

--- a/solution.py
+++ b/solution.py
@@ -187,10 +187,10 @@
     length, model = frames_ref.shape
     part_q, part_d, part_g = wq_ref.shape[1] // 2, model // 2, wg_ref.shape[1] // 4
     pieces = (
-        (0, 0, 2 * part_q, 50),
+        (0, 0, 2 * part_q, 66),
         (0, 2 * part_q, part_q, 66),
         (1, 0, part_d, 66),
-        (2, 0, part_g, 50),
+        (2, 0, part_g, 75),
         (2, part_g, part_g, 75),
         (3, 0, part_d, 66),
     )

time: 114 us -> 116 us (1.018)
  Pallas kernels: 111 us -> 113 us
    pallas_call x1, Pallas kernels: 111 us -> 113 us  [fused(): pl.pallas_call(functools.partial(block, n), out_shape=jax.ShapeDtypeStruc...]
where the time goes in v6:
time: 116 us
  Pallas kernels  113 us (97%)
  local copies, waits for them, and re-layouts  2.06 us (2%)
    pallas_call x1, Pallas kernels, fused(): pl.pallas_call(functools.partial(block, n), out_shape=jax.ShapeDtypeStruc...  113 us

profile of v6, /device:TPU:1, one launch (start us, length us, event | category | flops | bytes accessed | tf_op | source)
XLA Modules:
  0.0 115.5 jit_solution(9911791923630932451)
XLA Ops:
  0.7 112.8 %shard_map.136 = bf16[256,1536]{1,0:T(8,128)(2,1)} custom-call(bf16[256,1536]{1,0:T(8,128)(2,1)} %frames_ref.1, s32[1]{0:T(128)S(6)} %copy.16.count_ref, s32[1,4]{1,0:T(1,128)} %look_ref.1, f32[1536]{0:T(1024)} %gain_a_ref.1, bf16[96,768]{1,0:T(8,128)(2,1)} %wq_ref.1, bf16[96,768]{1,0:T(8,128)(2,1)} %wk_ref.1, bf16[96,768]{1,0:T(8,128)(2,1)} %wv_ref.1, ...), custom_call_target="tpu_custom_call" | custom-call | flops 4831838208 | bytes 18874368 | tf_op jit(solution)/shard_map/pallas_call | solution.py:569
  113.5 2.1 %copy.17 = bf16[256,1536]{1,0:T(8,128)(2,1)} copy(bf16[256,1536]{1,0:T(8,128)(2,1)} %shard_map.136) | data formatting | bytes 1572864

commit v7 on v5

--- a/solution.py
+++ b/solution.py
@@ -194,7 +194,7 @@
         (2, part_g, part_g, 75),
         (3, 0, part_d, 66),
     )
-    turns = (0, 0, 2, 3, 3, 4)
+    turns = (0, 0, 1, 2, 2, 3)
 
     def rows(p, owner, start, size):
         w, first = pieces[p][:2]

time: 114 us -> 114 us (level)
  no operation moved by 1% of the time
where the time goes in v7:
time: 114 us
  Pallas kernels  111 us (97%)
  local copies, waits for them, and re-layouts  2.06 us (2%)
    pallas_call x1, Pallas kernels, fused(): pl.pallas_call(functools.partial(block, n), out_shape=jax.ShapeDtypeStruc...  111 us

profile of v7, /device:TPU:1, one launch (start us, length us, event | category | flops | bytes accessed | tf_op | source)
XLA Modules:
  0.0 113.6 jit_solution(5188293541416900048)
XLA Ops:
  0.7 110.9 %shard_map.136 = bf16[256,1536]{1,0:T(8,128)(2,1)} custom-call(bf16[256,1536]{1,0:T(8,128)(2,1)} %frames_ref.1, s32[1]{0:T(128)S(6)} %copy.16.count_ref, s32[1,4]{1,0:T(1,128)} %look_ref.1, f32[1536]{0:T(1024)} %gain_a_ref.1, bf16[96,768]{1,0:T(8,128)(2,1)} %wq_ref.1, bf16[96,768]{1,0:T(8,128)(2,1)} %wk_ref.1, bf16[96,768]{1,0:T(8,128)(2,1)} %wv_ref.1, ...), custom_call_target="tpu_custom_call" | custom-call | flops 4831838208 | bytes 18874368 | tf_op jit(solution)/shard_map/pallas_call | solution.py:569
  111.5 2.1 %copy.17 = bf16[256,1536]{1,0:T(8,128)(2,1)} copy(bf16[256,1536]{1,0:T(8,128)(2,1)} %shard_map.136) | data formatting | bytes 1572864
